TPU v7x, 512 devices: a whole 4x4x16 slice. The times are simulated.
512 devices in a mesh: lat: 16 (over z), lon: 16 (over x, y_lo, core), dp: 2 (over y_hi).
Axes of the slice: x: 4, y: 4 (y_hi: 2, y_lo: 2; y = y_hi * 2 + y_lo), z: 16, core: 2. Of those that a mesh axis runs over, the one named last changes fastest.
Arguments:
- input_field: bfloat16 [2, 64, 1024, 256], P('dp', 'lat', 'lon'), may hold values from -6 to 6
- cotangent: bfloat16 [2, 64, 1024, 256], P('dp', 'lat', 'lon'), may hold values from -6 to 6
- channel_weight: bfloat16 [9, 256, 256], replicated, may hold values from -0.125 to 0.125
- basis_filter: bfloat16 [9, 64, 3, 17], replicated, may hold values from -0.875 to 0.875
- reach_cols: int32 [64], replicated, may hold values from 1 to 8, as said below
Outputs:
- output_field: bfloat16 [2, 64, 1024, 256], P('dp', 'lat', 'lon')
- grad_input: bfloat16 [2, 64, 1024, 256], P('dp', 'lat', 'lon')
- grad_weight: bfloat16 [9, 256, 256], P(None, None, 'lon')
Inputs may be any that keep to these rules, and one draw needn't show every extreme that they name: reach_cols is 8 at the first and the last row of the grid.
All inputs are finite; a program needn't handle non-finite values.
Results may differ from a plain program's by a relative error of at most 0.005.
Values may be sent and summed in bfloat16 or wider, within the bound.
A program may use at most 128 MiB of HBM per device.

v0:
```python
import math

import jax
import jax.numpy as jnp
from jax import lax
from jax.sharding import PartitionSpec as P


def padded(block, sides, width, periodic):
    for axis, dim in sides:
        count = lax.axis_size(axis)
        forward = [(i, i + 1) for i in range(count - 1)]
        if periodic:
            forward.append((count - 1, 0))
        backward = [(target, source) for source, target in forward]
        low = lax.ppermute(
            lax.slice_in_dim(block, block.shape[dim] - width, None, axis=dim), axis, forward
        )
        high = lax.ppermute(lax.slice_in_dim(block, 0, width, axis=dim), axis, backward)
        block = jnp.concatenate([low, block, high], axis=dim)
    return block


def masked_filter(basis_filter, reach_cols, lon_reach):
    tap_count = basis_filter.shape[3]
    offsets = jnp.abs(jnp.arange(tap_count, dtype=jnp.int32) - lon_reach)
    inside = (offsets[None, :] <= reach_cols[:, None]).astype(basis_filter.dtype)
    return basis_filter * inside[None, :, None, :]


def diagonal_table(tap_count, wide_cols, sector_cols):
    spread = (
        jnp.arange(wide_cols, dtype=jnp.int32)[:, None]
        - jnp.arange(sector_cols, dtype=jnp.int32)[None, :]
    )
    return (spread[None, :, :] == jnp.arange(tap_count, dtype=jnp.int32)[:, None, None]).astype(
        jnp.bfloat16
    )


def on_device(input_field, cotangent, channel_weight, basis_filter, reach_cols):
    batch_size, band_rows, sector_cols, channels = input_field.shape
    basis_count, total_rows, span_count, tap_count = basis_filter.shape
    lat_reach = span_count // 2
    lon_reach = tap_count // 2
    wide_cols = sector_cols + 2 * lon_reach
    diagonals = diagonal_table(tap_count, wide_cols, sector_cols)
    coeff_full = masked_filter(basis_filter, reach_cols, lon_reach)
    coeff_padded = jnp.pad(coeff_full, ((0, 0), (lat_reach, lat_reach), (0, 0), (0, 0)))
    first_row = lax.axis_index("lat") * band_rows
    beside_all = lax.dynamic_slice_in_dim(coeff_padded, first_row, band_rows + 2 * lat_reach, 1)
    own_rows = beside_all[:, lat_reach : lat_reach + band_rows]
    forward_band = jnp.einsum(
        "kiae,emj->aimkj", own_rows, diagonals, preferred_element_type=jnp.float32
    )
    forward_band = forward_band.astype(jnp.bfloat16).reshape(
        span_count, band_rows, wide_cols, basis_count * sector_cols
    )
    tall_field = padded(input_field, (("lat", 1),), lat_reach, False)
    framed_field = padded(tall_field, (("lon", 2),), lon_reach, True)
    mixed_sum = jnp.zeros((batch_size, band_rows, basis_count * sector_cols, channels), jnp.float32)
    for offset in range(span_count):
        mixed_sum = mixed_sum + jnp.einsum(
            "ims,bimc->bisc",
            forward_band[offset],
            framed_field[:, offset : offset + band_rows],
            preferred_element_type=jnp.float32,
        )
    convolved = mixed_sum.astype(jnp.bfloat16).reshape(
        batch_size, band_rows, basis_count, sector_cols, channels
    )
    output_field = jnp.einsum(
        "bikjc,kcd->bijd", convolved, channel_weight, preferred_element_type=jnp.float32
    ).astype(jnp.bfloat16)
    weight_terms = jnp.einsum(
        "bikjc,bijd->kcd", convolved, cotangent, preferred_element_type=jnp.float32
    )
    lon_count = lax.axis_size("lon")
    lat_count = lax.axis_size("lat")
    weight_part = lax.psum_scatter(weight_terms, "lon", scatter_dimension=2, tiled=True)
    weight_whole = lax.psum(weight_part, ("lat", "dp"))
    cell_count = batch_size * band_rows * sector_cols * lax.axis_size("dp") * lat_count * lon_count
    grad_weight = (weight_whole * (1.0 / math.sqrt(cell_count))).astype(jnp.bfloat16)
    local_products = jnp.einsum(
        "bijd,kcd->bikjc", cotangent, channel_weight, preferred_element_type=jnp.float32
    ).astype(jnp.bfloat16)
    product_tall = padded(local_products, (("lat", 1),), lat_reach, False)
    framed_products = padded(product_tall, (("lon", 3),), lon_reach, True)
    adjoint_coeff = jnp.stack(
        [
            beside_all[:, 2 * lat_reach - offset : 2 * lat_reach - offset + band_rows, offset]
            for offset in range(span_count)
        ],
        axis=2,
    )
    reversed_coeff = adjoint_coeff[..., ::-1]
    adjoint_band = jnp.einsum(
        "kpae,emq->apqkm", reversed_coeff, diagonals, preferred_element_type=jnp.float32
    )
    adjoint_band = adjoint_band.astype(jnp.bfloat16).reshape(
        span_count, band_rows, sector_cols, basis_count * wide_cols
    )
    gathered_sum = jnp.zeros((batch_size, band_rows, sector_cols, channels), jnp.float32)
    for offset in range(span_count):
        start_row = 2 * lat_reach - offset
        piece_rows = framed_products[:, start_row : start_row + band_rows].reshape(
            batch_size, band_rows, basis_count * wide_cols, channels
        )
        gathered_sum = gathered_sum + jnp.einsum(
            "pqr,bprc->bpqc", adjoint_band[offset], piece_rows, preferred_element_type=jnp.float32
        )
    grad_input = gathered_sum.astype(jnp.bfloat16)
    return (output_field, grad_input, grad_weight)


def solution(mesh):
    placed = (P("dp", "lat", "lon", None), P("dp", "lat", "lon", None), P(), P(), P())
    return jax.shard_map(
        on_device,
        mesh=mesh,
        in_specs=placed,
        out_specs=(P("dp", "lat", "lon", None), P("dp", "lat", "lon", None), P(None, None, "lon")),
        check_vma=False,
    )
```

profile of v0, /device:TPU:6, one launch (start us, length us, event | category | flops | bytes accessed | tf_op | source)
XLA Modules:
  0.0 421.2 jit_solution(2301171159127535775)
XLA Ops:
  7.2 0.0 copy-start
  7.2 0.0 reduce-scatter.2.cloned.1.call-start
  7.2 0.9 fusion.33
  8.1 3.8 collective-permute-start
  11.9 1.3 collective-permute-start.1
  13.2 0.0 copy-start.6
  13.3 1.6 copy.13
  14.8 0.7 compare_convert_fusion
  15.6 0.1 broadcast_multiply_fusion
  15.7 0.0 copy-start.7
  15.7 1.0 convert_bitcast_fusion.1
  16.7 0.0 collective-permute-done
  16.7 0.0 copy-done.7
  16.7 1.0 collective-permute-done.1
  17.7 1.9 collective-permute-start.2
  19.7 4.5 %collective-permute-start.3 = (bf16[1,6,8,256]{3,2,1,0:T(8,128)(2,1)S(1)}, bf16[1,6,8,256]{3,2,1,0:T(8,128)(2,1)S(1)}, u32[]{:S(2)}, u32[]{:S(2)}) collective-permute-start(bf16[1,6,8,256]{3,2,1,0:T(8,128)(2,1)S(1)} %get-tuple-element.20), channel_id=1, source_target_pairs={{2,0},{4,2},{6,4},{8,6},{10,8},{12,10},{14,12},{16,14},{18,16},{20... | collective-permute-start | bytes 73736 | tf_op jit(solution)/shard_map/ppermute | solution.py:19
  24.2 1.0 fusion.29
  25.2 0.4 copy.16
  25.6 0.4 copy.14
  26.1 0.4 copy.18
  26.5 0.0 collective-permute-done.2
  26.5 0.0 collective-permute-done.3
  26.5 0.4 fusion.20
  27.0 0.4 fusion.21
  27.4 0.0 copy-start.5
  27.4 0.4 add_convert_fusion
  27.9 0.4 copy-done.5
  28.3 2.0 convolution_bitcast_fusion
  30.3 0.0 reduce-scatter.2.cloned.1.call-update
  30.3 0.0 all-reduce.3.cloned.1.call-start
  30.4 0.0 copy-done
  30.4 1.4 fusion
  31.8 0.9 fusion.31
  32.7 4.5 %collective-permute-start.4 = (bf16[1,1,9,64,256]{4,3,1,2,0:T(8,128)(2,1)}, bf16[1,1,9,64,256]{4,3,1,2,0:T(8,128)(2,1)}, u32[]{:S(2)}, u32[]{:S(2)}) collective-permute-start(bf16[1,1,9,64,256]{4,3,1,2,0:T(8,128)(2,1)} %get-tuple-element.14), channel_id=1, source_target_pairs={{0,32},{32,64},{64,96},{96,128},{128,160},{160,192},{192,224},{224... | collective-permute-start | bytes 884744 | tf_op jit(solution)/shard_map/ppermute | solution.py:16
  37.2 1.3 collective-permute-start.5
  38.5 0.8 pad_dynamic-slice_fusion.1
  39.3 0.6 pad_maximum_fusion.5
  39.9 1.5 rev.3
  41.4 1.8 convert_bitcast_fusion
  43.2 2.1 fusion.28
  45.3 2.6 copy.24
  47.9 2.5 copy.21
  50.4 2.5 copy.27
  52.9 0.0 collective-permute-done.4
  52.9 0.0 collective-permute-done.5
  52.9 0.9 pad_maximum_fusion.4
  53.8 1.9 collective-permute-start.6
  55.7 4.5 %collective-permute-start.7 = (bf16[1,6,9,8,256]{4,3,1,2,0:T(8,128)(2,1)S(1)}, bf16[1,6,9,8,256]{4,3,1,2,0:T(8,128)(2,1)S(1)}, u32[]{:S(2)}, u32[]{:S(2)}) collective-permute-start(bf16[1,6,9,8,256]{4,3,1,2,0:T(8,128)(2,1)S(1)} %get-tuple-element.13), channel_id=1, source_target_pairs={{2,0},{4,2},{6,4},{8,6},{10,8},{12,10},{14,12},{16,14},{18,16},{20... | collective-permute-start | bytes 663560 | tf_op jit(solution)/shard_map/ppermute | solution.py:19
  60.3 1.1 fusion.11
  61.4 1.4 collective-permute-done.6
  62.8 1.7 collective-permute-done.7
  64.5 1.5 pad_maximum_fusion
  66.0 0.4 fusion.30
  66.4 0.1 copy.23
  66.5 0.1 copy.20
  66.6 0.1 copy.26
  66.7 1.0 copy-done.2
  67.7 0.4 fusion.34
  68.2 1.1 convolution_add_fusion.1
  69.3 32.1 %reduce-scatter.2.cloned.1.call-done = f32[9,256,16]{1,2,0:T(8,128)} async-done(((f32[9,256,256]{1,2,0:T(8,128)}), f32[9,256,16]{1,2,0:T(8,128)}) %reduce-scatter.2.cloned.1.call-update) | async-done | bytes 147472 | tf_op jit(solution)/shard_map/reduce_scatter | solution.py:80
  101.4 0.0 all-reduce.3.cloned.1.call-update
  101.4 2.0 fusion.14
  103.4 309.4 %all-reduce.3.cloned.1.call-done = f32[9,256,16]{1,2,0:T(8,128)} async-done(((f32[9,256,16]{1,2,0:T(8,128)}), f32[9,256,16]{1,2,0:T(8,128)}) %all-reduce.3.cloned.1.call-update) | async-done | bytes 147472 | tf_op jit(solution)/shard_map/psum | solution.py:81
  412.8 1.6 multiply_convert_fusion
  (15 shorter events, 0.1 us)
Async XLA Ops:
  7.2 23.2 %copy-start = (bf16[9,256,256]{2,1,0:T(8,128)(2,1)S(1)}, bf16[9,256,256]{2,1,0:T(8,128)(2,1)}, u32[]{:S(2)}) copy-start(bf16[9,256,256]{2,1,0:T(8,128)(2,1)} %param.7) | copy-start | bytes 3538948
  7.2 94.2 %reduce-scatter.2.cloned.1.call-start = ((), (), s32[]{:S(2)}) async-start(), calls=%async_computation.1 | async-start | bytes 2506752 | tf_op jit(solution)/shard_map/reduce_scatter | solution.py:80
  8.1 8.6 %collective-permute-start = (bf16[1,1,64,256]{3,2,1,0:T(8,128)(2,1)S(1)}, bf16[1,1,64,256]{3,2,1,0:T(8,128)(2,1)S(1)}, u32[]{:S(2)}, u32[]{:S(2)}) collective-permute-start(bf16[1,1,64,256]{3,2,1,0:T(8,128)(2,1)S(1)} %get-tuple-element.22), channel_id=1, source_target_pairs={{0,32},{32,64},{64,96},{96,128},{128,160},{160,192},{192,224},{224... | collective-permute-start | bytes 98312 | tf_op jit(solution)/shard_map/ppermute | solution.py:16
  11.9 5.8 %collective-permute-start.1 = (bf16[1,1,64,256]{3,2,1,0:T(8,128)(2,1)S(1)}, bf16[1,1,64,256]{3,2,1,0:T(8,128)(2,1)S(1)}, u32[]{:S(2)}, u32[]{:S(2)}) collective-permute-start(bf16[1,1,64,256]{3,2,1,0:T(8,128)(2,1)S(1)} %get-tuple-element.21), channel_id=1, source_target_pairs={{32,0},{64,32},{96,64},{128,96},{160,128},{192,160},{224,192},{256... | collective-permute-start | bytes 98312 | tf_op jit(solution)/shard_map/ppermute | solution.py:19
  13.2 3.4 copy-start.6
  15.6 1.0 copy-start.1
  15.7 1.0 copy-start.7
  17.7 8.8 %collective-permute-start.2 = (bf16[1,6,8,256]{3,2,1,0:T(8,128)(2,1)S(1)}, bf16[1,6,8,256]{3,2,1,0:T(8,128)(2,1)S(1)}, u32[]{:S(2)}, u32[]{:S(2)}) collective-permute-start(bf16[1,6,8,256]{3,2,1,0:T(8,128)(2,1)S(1)} %get-tuple-element.19), channel_id=1, source_target_pairs={{0,2},{2,4},{4,6},{6,8},{8,10},{10,12},{12,14},{14,16},{16,18},{18... | collective-permute-start | bytes 73736 | tf_op jit(solution)/shard_map/ppermute | solution.py:16
  19.7 6.9 %collective-permute-start.3 = (bf16[1,6,8,256]{3,2,1,0:T(8,128)(2,1)S(1)}, bf16[1,6,8,256]{3,2,1,0:T(8,128)(2,1)S(1)}, u32[]{:S(2)}, u32[]{:S(2)}) collective-permute-start(bf16[1,6,8,256]{3,2,1,0:T(8,128)(2,1)S(1)} %get-tuple-element.20), channel_id=1, source_target_pairs={{2,0},{4,2},{6,4},{8,6},{10,8},{12,10},{14,12},{16,14},{18,16},{20... | collective-permute-start | bytes 73736 | tf_op jit(solution)/shard_map/ppermute | solution.py:19
  27.4 0.9 copy-start.5
  30.3 382.5 %all-reduce.3.cloned.1.call-start = ((), (), s32[]{:S(2)}) async-start(), calls=%async_computation.2 | async-start | bytes 294912 | tf_op jit(solution)/shard_map/psum | solution.py:81
  32.7 20.3 %collective-permute-start.4 = (bf16[1,1,9,64,256]{4,3,1,2,0:T(8,128)(2,1)}, bf16[1,1,9,64,256]{4,3,1,2,0:T(8,128)(2,1)}, u32[]{:S(2)}, u32[]{:S(2)}) collective-permute-start(bf16[1,1,9,64,256]{4,3,1,2,0:T(8,128)(2,1)} %get-tuple-element.14), channel_id=1, source_target_pairs={{0,32},{32,64},{64,96},{96,128},{128,160},{160,192},{192,224},{224... | collective-permute-start | bytes 884744 | tf_op jit(solution)/shard_map/ppermute | solution.py:16
  37.2 15.7 %collective-permute-start.5 = (bf16[1,1,9,64,256]{4,3,1,2,0:T(8,128)(2,1)}, bf16[1,1,9,64,256]{4,3,1,2,0:T(8,128)(2,1)}, u32[]{:S(2)}, u32[]{:S(2)}) collective-permute-start(bf16[1,1,9,64,256]{4,3,1,2,0:T(8,128)(2,1)} %get-tuple-element.15), channel_id=1, source_target_pairs={{32,0},{64,32},{96,64},{128,96},{160,128},{192,160},{224,192},{256... | collective-permute-start | bytes 884744 | tf_op jit(solution)/shard_map/ppermute | solution.py:19
  53.8 9.0 %collective-permute-start.6 = (bf16[1,6,9,8,256]{4,3,1,2,0:T(8,128)(2,1)S(1)}, bf16[1,6,9,8,256]{4,3,1,2,0:T(8,128)(2,1)S(1)}, u32[]{:S(2)}, u32[]{:S(2)}) collective-permute-start(bf16[1,6,9,8,256]{4,3,1,2,0:T(8,128)(2,1)S(1)} %get-tuple-element.12), channel_id=1, source_target_pairs={{0,2},{2,4},{4,6},{6,8},{8,10},{10,12},{12,14},{14,16},{16,18},{18... | collective-permute-start | bytes 663560 | tf_op jit(solution)/shard_map/ppermute | solution.py:16
  55.7 8.8 %collective-permute-start.7 = (bf16[1,6,9,8,256]{4,3,1,2,0:T(8,128)(2,1)S(1)}, bf16[1,6,9,8,256]{4,3,1,2,0:T(8,128)(2,1)S(1)}, u32[]{:S(2)}, u32[]{:S(2)}) collective-permute-start(bf16[1,6,9,8,256]{4,3,1,2,0:T(8,128)(2,1)S(1)} %get-tuple-element.13), channel_id=1, source_target_pairs={{2,0},{4,2},{6,4},{8,6},{10,8},{12,10},{14,12},{16,14},{18,16},{20... | collective-permute-start | bytes 663560 | tf_op jit(solution)/shard_map/ppermute | solution.py:19
  66.6 1.1 copy-start.2
  66.7 1.4 copy-start.4
  68.1 33.2 %copy-start.3 = (bf16[1,4,64,9,80]{2,4,3,1,0:T(8,128)(2,1)S(1)}, bf16[1,4,64,9,80]{2,4,3,1,0:T(8,128)(2,1)}, u32[]{:S(2)}) copy-start(bf16[1,4,64,9,80]{2,4,3,1,0:T(8,128)(2,1)} %copy.27) | copy-start | bytes 1105924
Sparse Core Ops, SparseCore 0:
  30.4 70.8 reduce-scatter.1
  104.3 308.4 all-reduce.2
where the time goes:
time: 422 us; the launch traced here: 421 us
  waiting for transfers between devices  346 us (82%)
  starting transfers between devices  23.9 us (6%)
  local copies, waits for them, and re-layouts  19.8 us (5%)
  between operations  14.4 us (3%)
  matrix products  12.1 us (3%)
  other arithmetic  5.37 us (1%)
    psum x1, waiting for transfers between devices, on_device(): weight_whole = lax.psum(weight_part, ('lat', 'dp'))  309 us
    reduce_scatter x1, waiting for transfers between devices, on_device(): lax.psum_scatter(weight_terms, 'lon', scatter_dimension=2, tiled=True)  32.1 us
    ppermute x4, starting transfers between devices, padded(): lax.ppermute(lax.slice_in_dim(block, block.shape[dim] - width, None, axis...  12.2 us
    ppermute x4, starting transfers between devices, padded(): lax.ppermute(lax.slice_in_dim(block, 0, width, axis=dim), axis, backward)  11.7 us
    slice x4, local copies, waits for them, and re-layouts, on_device(): adjoint_band[offset]  9.72 us
  transfers between devices with their start and end apart: 10, of which 5 were waited for; matrix products, arithmetic and copies ran while one was open for 7% of the time, Pallas kernels for 0%

commit v1 on v0

v1 whole, which is shorter than its diff:
```python
import functools
import math

import jax
import jax.numpy as jnp
from jax import lax
from jax.experimental import pallas as pl
from jax.experimental.pallas import tpu as pltpu
from jax.sharding import PartitionSpec as P

MESH = pl.DeviceIdType.MESH
F32 = jnp.float32
BF16 = jnp.bfloat16


def kernel_body(sizes, coeff_ref, field_hbm, cot_hbm, weight_hbm, out_hbm, gin_hbm, gw_hbm,
                win, edge, weight, fband, bband, conv, cot_t, a_send, a_recv, b_send, b_recv,
                c_send, final, out_v, gin_v, local_sem, halo_send, halo_recv,
                a_ssem, a_rsem, b_ssem, b_rsem, c_ssem, c_rsem):
    nz, nlon, ndp, basis, rows, cols, chans, taps = sizes
    reach = taps // 2
    nq = nlon // 2
    blk = chans // nlon
    scale = 1.0 / math.sqrt(ndp * nz * rows * nlon * cols)
    z = lax.axis_index("lat")
    lon = lax.axis_index("lon")
    dp = lax.axis_index("dp")
    q = lon // 2
    core = lon % 2
    mate = q * 2 + 1 - core
    block = cols + 2 * reach
    side = 2 * reach
    halves = 2
    half = chans // halves

    loads = []
    for n, src in enumerate((field_hbm, cot_hbm)):
        loads.append(pltpu.make_async_copy(
            src.at[0], win.at[n, core, pl.ds(1, rows), pl.ds(side, cols)], local_sem.at[n]))
    loads.append(pltpu.make_async_copy(weight_hbm, weight, local_sem.at[2]))
    for load in loads:
        load.start()

    barrier = pltpu.get_barrier_semaphore()
    signals = 0

    def greet(zz, ll, dd):
        pl.semaphore_signal(barrier, inc=1, device_id={"lat": zz, "lon": ll, "dp": dd},
                            device_id_type=MESH)

    up = lax.rem(z + 1, nz)
    down = lax.rem(z + nz - 1, nz)
    q_next = lax.rem(q + 1, nq)
    q_prev = lax.rem(q + nq - 1, nq)
    greet(z, mate, dp)
    signals += 1
    for zz in (down, up):
        for cc in range(2):
            greet(zz, q * 2 + cc, dp)
            signals += 1
    for zz in (down, z, up):
        greet(zz, q_prev * 2 + 1, dp)
        greet(zz, q_next * 2, dp)
        signals += 2
    for r in range(1, nq):
        greet(z, lax.rem(q + r, nq) * 2 + core, dp)
        signals += 1
    for r in range(1, nz * ndp):
        place = lax.rem(dp * nz + z + r, nz * ndp)
        greet(lax.rem(place, nz), lon, place // nz)
        signals += 1

    lanes = 3 * block + side
    tap_lane = lax.broadcasted_iota(jnp.int32, (128, lanes), 0)
    out_lane = lax.broadcasted_iota(jnp.int32, (128, lanes), 1)

    def make_band(dst, transposed):
        rowvec = jnp.zeros((rows * 16, lanes), F32)
        for a in range(3):
            if transposed:
                picked = coeff_ref[2 - a, pl.ds(16 * a, rows * 16), :]
                hit = (out_lane == reach + block * a + (taps - 1) - tap_lane) & (tap_lane < taps)
            else:
                picked = coeff_ref[a, pl.ds(16, rows * 16), :]
                hit = (out_lane == reach + block * a + tap_lane) & (tap_lane < taps)
            rowvec = rowvec + jnp.dot(picked, jnp.where(hit, 1.0, 0.0).astype(BF16),
                                      preferred_element_type=F32)
        for i in range(rows):
            for k in range(basis):
                row = jnp.broadcast_to(rowvec[i * 16 + k:i * 16 + k + 1, :], (cols, lanes))
                dst[i, pl.ds(k * cols, cols), :] = pltpu.roll(
                    row, 0, 1, stride=1, stride_axis=0).astype(BF16)

    make_band(fband, False)

    pl.semaphore_wait(barrier, signals)

    far = lax.rem(q + nq - 1 + 2 * core, nq)
    started = []

    def send(src, dst, slot, zz, ll):
        copy = pltpu.make_async_remote_copy(
            src_ref=src, dst_ref=dst, send_sem=halo_send.at[slot[0]], recv_sem=halo_recv.at[slot[1]],
            device_id={"lat": zz, "lon": ll, "dp": dp}, device_id_type=MESH)
        copy.start()
        started.append(copy)

    for n, src in enumerate((field_hbm, cot_hbm)):
        base = n * 11
        for zz, row, place, which in ((up, rows - 1, 0, 0), (down, 0, rows + 1, 1)):
            for cc in range(2):
                send(src.at[0, row], win.at[n, core, place, pl.ds(side, cols)],
                     (base + which * 2 + cc, base + which * 2 + core), zz, q * 2 + cc)
        edge_cols = pl.ds(pl.multiple_of(core * (cols - side), 16), side)
        for cc in range(2):
            send(src.at[0, :, edge_cols], edge.at[n, 1 - core, pl.ds(1, rows)],
                 (base + 4 + cc, base + 4 + 1 - core), z, far * 2 + cc)
        for zz, row, place, which in ((up, rows - 1, 0, 0), (down, 0, rows + 1, 1)):
            for cc in range(2):
                send(src.at[0, row, edge_cols], edge.at[n, 1 - core, place],
                     (base + 6 + which * 2 + cc, base + 6 + which * 2 + 1 - core), zz, far * 2 + cc)
        send(src.at[0], win.at[n, core, pl.ds(1, rows), pl.ds(side, cols)],
             (base + 10, base + 10), z, mate)

    make_band(bband, True)

    for load in loads:
        load.wait()
    for n in range(2):
        base = n * 11
        row_like = win.at[n, 0, 0, pl.ds(side, cols)]
        for s in range(4):
            pltpu.make_async_copy(row_like, row_like, halo_recv.at[base + s]).wait()
        edge_like = edge.at[n, 0, pl.ds(1, rows)]
        for s in range(4, 6):
            pltpu.make_async_copy(edge_like, edge_like, halo_recv.at[base + s]).wait()
        corner_like = edge.at[n, 0, 0]
        for s in range(6, 10):
            pltpu.make_async_copy(corner_like, corner_like, halo_recv.at[base + s]).wait()
        all_like = win.at[n, 0, pl.ds(1, rows), pl.ds(side, cols)]
        pltpu.make_async_copy(all_like, all_like, halo_recv.at[base + 10]).wait()

    def blank(place):
        for n in range(2):
            for s in range(2):
                win[n, s, place, pl.ds(side, cols), :] = jnp.zeros((cols, chans), BF16)
                edge[n, s, place] = jnp.zeros((side, chans), BF16)

    @pl.when(z == 0)
    def _():
        blank(0)

    @pl.when(z == nz - 1)
    def _():
        blank(rows + 1)

    first_half = lax.broadcasted_iota(jnp.int32, (side, chans), 0) < reach
    nothing = jnp.zeros((side, chans), F32)
    for n in range(2):
        for s in range(2):
            for r in range(rows + 3):
                if r == 0:
                    before = nothing
                elif s == 0:
                    before = win[n, 1, r - 1, pl.ds(side, side), :].astype(F32)
                else:
                    before = edge[n, 1, r - 1].astype(F32)
                if r == rows + 2:
                    after = nothing
                elif s == 0:
                    after = edge[n, 0, r].astype(F32)
                else:
                    after = win[n, 0, r, pl.ds(cols, side), :].astype(F32)
                win[n, s, r, pl.ds(0, side), :] = jnp.where(first_half, before, after).astype(BF16)

    def window(n, s, i):
        return jnp.concatenate(
            [win[n, s, i], win[n, s, i + 1], win[n, s, i + 2], win[n, s, i + 3, pl.ds(0, side), :]],
            axis=0)

    for s in range(2):
        for i in range(rows):
            part = jnp.dot(fband[i], window(0, s, i), preferred_element_type=F32)
            conv[:, s * rows + i] = part.astype(BF16).reshape(basis, cols, chans)

    for s in range(2):
        for i in range(rows):
            row = win[1, s, i + 1, pl.ds(side, cols), :].astype(F32)
            if i % 2 == 0:
                held = row
            else:
                pair = jnp.concatenate([held, row], axis=0)
                cot_t[:, :, :, pl.ds((s * rows + i - 1) * cols, 2 * cols)] = pair.T.astype(
                    BF16).reshape(nq, 2, blk, 2 * cols)

    mine_t = cot_t[:, core].reshape(nq * blk, 2 * rows * cols)
    for k in range(basis):
        terms = jnp.dot(mine_t, conv[k].reshape(2 * rows * cols, chans), preferred_element_type=F32)
        a_send[:, k] = terms.astype(BF16).reshape(nq, blk, chans)

    a_copies = []
    for r in range(1, nq):
        to = lax.rem(q + r, nq)
        copy = pltpu.make_async_remote_copy(
            src_ref=a_send.at[to], dst_ref=a_recv.at[r - 1], send_sem=a_ssem.at[r - 1],
            recv_sem=a_rsem.at[r - 1],
            device_id={"lat": z, "lon": to * 2 + core, "dp": dp}, device_id_type=MESH)
        copy.start()
        a_copies.append(copy)

    total = jnp.zeros((rows * cols, chans), F32)
    for k in range(basis):
        own = conv[k, pl.ds(core * rows, rows)].reshape(rows * cols, chans)
        total = total + jnp.dot(own, weight[k], preferred_element_type=F32)
    out_v[...] = total.astype(BF16).reshape(rows, cols, chans)
    out_copy = pltpu.make_async_copy(out_v, out_hbm.at[0], local_sem.at[0])
    out_copy.start()

    for i in range(rows):
        wide = jnp.concatenate(
            [win[1, core, i], win[1, core, i + 1], win[1, core, i + 2],
             win[1, core, i + 3, pl.ds(0, side), :]], axis=0)
        part = jnp.dot(bband[i], wide, preferred_element_type=F32)
        conv[:, i] = part.astype(BF16).reshape(basis, cols, chans)
    total = jnp.zeros((rows * cols, chans), F32)
    for k in range(basis):
        own = conv[k, pl.ds(0, rows)].reshape(rows * cols, chans)
        total = total + lax.dot_general(own, weight[k], (((1,), (1,)), ((), ())),
                                        preferred_element_type=F32)
    gin_v[...] = total.astype(BF16).reshape(rows, cols, chans)
    gin_copy = pltpu.make_async_copy(gin_v, gin_hbm.at[0], local_sem.at[1])
    gin_copy.start()

    for copy in a_copies:
        copy.wait_recv()
    for k in range(basis):
        summed = a_send[q, k].astype(F32)
        for r in range(nq - 1):
            summed = summed + a_recv[r, k].astype(F32)
        b_send[k] = summed.astype(BF16)

    def keeper(k):
        return (nz * k) // basis

    def tile(ref, k, h):
        return ref.at[k, :, pl.ds(h * half, half)]

    me = dp * nz + z
    for k in range(basis):
        for h in range(halves):
            away = jnp.logical_or(z != keeper(k), dp != h)

            @pl.when(away)
            def _(k=k, h=h):
                pltpu.make_async_remote_copy(
                    src_ref=tile(b_send, k, h), dst_ref=b_recv.at[me],
                    send_sem=b_ssem.at[k * halves + h], recv_sem=b_rsem.at[me],
                    device_id={"lat": keeper(k), "lon": lon, "dp": h}, device_id_type=MESH).start()

    my_k = (basis * z + nz - 1) // nz
    keeps = jnp.logical_and(my_k < basis, (nz * my_k) // basis == z)
    my_k = jnp.minimum(my_k, basis - 1)
    my_lanes = pl.ds(pl.multiple_of(dp * half, half), half)

    @pl.when(keeps)
    def _():
        for r in range(1, nz * ndp):
            place = lax.rem(me + r, nz * ndp)
            pltpu.make_async_copy(b_recv.at[place], b_recv.at[place], b_rsem.at[place]).wait()
        b_recv[me] = b_send[my_k, :, my_lanes]
        summed = jnp.zeros((blk, half), F32)
        for r in range(nz * ndp):
            summed = summed + b_recv[r].astype(F32)
        c_send[...] = (summed * scale).astype(BF16)
        for r in range(1, nz * ndp):
            place = lax.rem(me + r, nz * ndp)
            pltpu.make_async_remote_copy(
                src_ref=c_send, dst_ref=final.at[my_k, :, my_lanes],
                send_sem=c_ssem.at[r], recv_sem=c_rsem.at[my_k * halves + dp],
                device_id={"lat": lax.rem(place, nz), "lon": lon, "dp": place // nz},
                device_id_type=MESH).start()
        final[my_k, :, my_lanes] = c_send[...]

    for k in range(basis):
        for h in range(halves):
            away = jnp.logical_or(z != keeper(k), dp != h)

            @pl.when(away)
            def _(k=k, h=h):
                spot = tile(final, k, h)
                pltpu.make_async_copy(spot, spot, c_rsem.at[k * halves + h]).wait()

    gw_copy = pltpu.make_async_copy(final, gw_hbm, local_sem.at[2])
    gw_copy.start()

    for copy in started:
        copy.wait_send()
    for copy in a_copies:
        copy.wait_send()
    for k in range(basis):
        for h in range(halves):
            away = jnp.logical_or(z != keeper(k), dp != h)

            @pl.when(away)
            def _(k=k, h=h):
                spot = tile(b_send, k, h)
                pltpu.make_async_copy(spot, spot, b_ssem.at[k * halves + h]).wait()

    @pl.when(keeps)
    def _():
        for r in range(1, nz * ndp):
            pltpu.make_async_copy(c_send, c_send, c_ssem.at[r]).wait()

    out_copy.wait()
    gin_copy.wait()
    gw_copy.wait()


def on_device(input_field, cotangent, channel_weight, basis_filter, reach_cols):
    _, rows, cols, chans = input_field.shape
    basis, nlat, spans, taps = basis_filter.shape
    reach = taps // 2
    nz, nlon, ndp = (lax.axis_size(name) for name in ("lat", "lon", "dp"))
    nq = nlon // 2
    blk = chans // nlon
    block = cols + 2 * reach
    side = 2 * reach
    lanes = spans * block + side

    first = lax.axis_index("lat") * rows
    offsets = jnp.abs(jnp.arange(taps, dtype=jnp.int32) - reach)
    near = lax.dynamic_slice_in_dim(jnp.pad(basis_filter, ((0, 0), (1, 1), (0, 0), (0, 0))),
                                    first, rows + 2, 1)
    near_reach = lax.dynamic_slice_in_dim(jnp.pad(reach_cols, (1, 1)), first, rows + 2, 0)
    inside = offsets[None, :] <= near_reach[:, None]
    near = jnp.where(inside[None, :, None, :], near, 0)
    coeff = jnp.transpose(near, (2, 1, 0, 3))
    coeff = jnp.pad(coeff, ((0, 0), (0, 0), (0, 16 - basis), (0, 128 - taps)))
    coeff = coeff.reshape(spans, (rows + 2) * 16, 128).astype(BF16)

    sizes = (nz, nlon, ndp, basis, rows, cols, chans, taps)
    vmem = pl.BlockSpec(memory_space=pltpu.VMEM)
    anywhere = pl.BlockSpec(memory_space=pl.ANY)
    dma = pltpu.SemaphoreType.DMA
    group = nz * ndp
    out, gin, gw = pl.pallas_call(
        functools.partial(kernel_body, sizes),
        out_shape=(jax.ShapeDtypeStruct(input_field.shape, BF16),
                   jax.ShapeDtypeStruct(input_field.shape, BF16),
                   jax.ShapeDtypeStruct((basis, blk, chans), BF16)),
        in_specs=[vmem, anywhere, anywhere, anywhere],
        out_specs=(anywhere, anywhere, anywhere),
        scratch_shapes=[
            pltpu.VMEM((2, 2, rows + 3, block, chans), BF16),
            pltpu.VMEM((2, 2, rows + 2, side, chans), BF16),
            pltpu.VMEM((basis, chans, chans), BF16),
            pltpu.VMEM((rows, basis * cols, lanes), BF16),
            pltpu.VMEM((rows, basis * cols, lanes), BF16),
            pltpu.VMEM((basis, 2 * rows, cols, chans), BF16),
            pltpu.VMEM((nq, 2, blk, 2 * rows * cols), BF16),
            pltpu.VMEM((nq, basis, blk, chans), BF16),
            pltpu.VMEM((max(nq - 1, 1), basis, blk, chans), BF16),
            pltpu.VMEM((basis, blk, chans), BF16),
            pltpu.VMEM((group, blk, chans // 2), BF16),
            pltpu.VMEM((blk, chans // 2), BF16),
            pltpu.VMEM((basis, blk, chans), BF16),
            pltpu.VMEM((rows, cols, chans), BF16),
            pltpu.VMEM((rows, cols, chans), BF16),
            dma((3,)), dma((22,)), dma((22,)),
            dma((max(nq - 1, 1),)), dma((max(nq - 1, 1),)),
            dma((basis * 2,)), dma((group,)), dma((group,)), dma((basis * 2,)),
        ],
        compiler_params=pltpu.CompilerParams(
            collective_id=0, has_side_effects=True, vmem_limit_bytes=48 * 1024 * 1024),
        name="disco_block",
    )(coeff, input_field, cotangent, channel_weight)
    return out, gin, jnp.transpose(gw, (0, 2, 1))


def solution(mesh):
    placed = (P("dp", "lat", "lon", None), P("dp", "lat", "lon", None), P(), P(), P())
    return jax.shard_map(
        on_device,
        mesh=mesh,
        in_specs=placed,
        out_specs=(P("dp", "lat", "lon", None), P("dp", "lat", "lon", None), P(None, None, "lon")),
        check_vma=False,
    )
```

time: 422 us -> 63 us (0.15)
  the two profiles are of different devices: /device:TPU:6 before, /device:TPU:8 now
where the time goes in v1:
time: 63 us; the launch traced here: 62.8 us
  Pallas kernels  54.6 us (87%)
  local copies, waits for them, and re-layouts  6.23 us (10%)
  other arithmetic  1.25 us (2%)
  between operations  0.67 us (1%)
    pallas_call x1, Pallas kernels, on_device(): pl.pallas_call(functools.partial(kernel_body, sizes), out_shape=(jax.Shap...  54.6 us
    unnamed x10, local copies, waits for them, and re-layouts  5.46 us

profile of v1, /device:TPU:8, one launch (start us, length us, event | category | flops | bytes accessed | tf_op | source)
XLA Modules:
  0.0 62.8 jit_solution(3514114618817048527)
XLA Ops:
  0.6 0.7 %pad_dynamic-slice_fusion = s32[6]{0:T(128)S(1)} fusion(s32[]{:T(128)S(6)} %select_n.8, s32[64]{0:T(128)} %param.9), kind=kLoop, calls=%fused_computation.2 | loop fusion | bytes 284 | tf_op jit(solution)/shard_map/dynamic_slice | solution.py:334
  1.4 0.1 broadcast_compare_fusion
  1.5 1.2 %select_bitcast_fusion = bf16[3,6,9,17]{1,0,3,2:T(4,128)(2,1)S(1)} fusion(s32[]{:T(128)S(6)} %select_n.8, bf16[9,64,3,17]{1,2,3,0:T(4,128)(2,1)} %param.8, pred[6,17]{0,1:T(8,128)(4,1)S(1)} %broadcast_compare_fusion), kind=kLoop, calls=%fused_computation | loop fusion | flops 2754 | bytes 64366 | tf_op jit(solution)/shard_map/transpose | solution.py:337
  2.6 0.4 copy.9
  3.1 0.0 copy-start
  3.1 1.3 %copy-done = bf16[9,256,256]{2,1,0:T(8,128)(2,1)S(1)} copy-done((bf16[9,256,256]{2,1,0:T(8,128)(2,1)S(1)}, bf16[9,256,256]{2,1,0:T(8,128)(2,1)}, u32[]{:S(2)}) %copy-start) | copy-done | bytes 1179672
  4.4 0.0 copy-start.1
  4.4 0.9 %copy-done.1 = bf16[1,4,64,256]{3,2,1,0:T(8,128)(2,1)S(1)} copy-done((bf16[1,4,64,256]{3,2,1,0:T(8,128)(2,1)S(1)}, bf16[1,4,64,256]{3,2,1,0:T(8,128)(2,1)}, u32[]{:S(2)}) %copy-start.1) | copy-done | bytes 131096
  5.3 0.0 copy-start.2
  5.3 0.9 %copy-done.2 = bf16[1,4,64,256]{3,2,1,0:T(8,128)(2,1)S(1)} copy-done((bf16[1,4,64,256]{3,2,1,0:T(8,128)(2,1)S(1)}, bf16[1,4,64,256]{3,2,1,0:T(8,128)(2,1)}, u32[]{:S(2)}) %copy-start.2) | copy-done | bytes 131096
  6.2 54.6 %disco_block.1 = (bf16[1,4,64,256]{3,2,1,0:T(8,128)(2,1)S(1)}, bf16[1,4,64,256]{3,2,1,0:T(8,128)(2,1)S(1)}, bf16[9,16,256]{2,1,0:T(8,128)(2,1)S(1)}) custom-call(bf16[3,96,128]{2,1,0:T(8,128)(2,1)S(1)} %bitcast.4, bf16[1,4,64,256]{3,2,1,0:T(8,128)(2,1)S(1)} %copy-done.1, bf16[1,4,64,256]{3,2,1,0:T(8,128)(2,1)S(1)} %copy-done.2, bf16[9,256,256]{2,1,0:T(8,128)(2,1)S(1)} %copy-done), custom_call_target="tpu_custom_call" | custom-call | tf_op jit(solution)/shard_map/disco_block/pallas_call | solution.py:346
  60.8 0.7 %copy.13 = bf16[1,4,64,256]{3,2,1,0:T(8,128)(2,1)} copy(bf16[1,4,64,256]{3,2,1,0:T(8,128)(2,1)S(1)} %get-tuple-element.12) | data formatting | bytes 262144
  61.5 0.7 %copy.14 = bf16[1,4,64,256]{3,2,1,0:T(8,128)(2,1)} copy(bf16[1,4,64,256]{3,2,1,0:T(8,128)(2,1)S(1)} %get-tuple-element.13) | data formatting | bytes 262144
  62.2 0.6 %copy.15 = bf16[9,256,16]{1,2,0:T(8,128)(2,1)} copy(bf16[9,256,16]{1,2,0:T(8,128)(2,1)S(1)} %bitcast.5) | data formatting | bytes 147456
  (2 shorter events, 0.0 us)
Async XLA Ops:
  3.1 1.3 %copy-start = (bf16[9,256,256]{2,1,0:T(8,128)(2,1)S(1)}, bf16[9,256,256]{2,1,0:T(8,128)(2,1)}, u32[]{:S(2)}) copy-start(bf16[9,256,256]{2,1,0:T(8,128)(2,1)} %weight_hbm.1) | copy-start | bytes 3538948
  4.4 0.9 %copy-start.1 = (bf16[1,4,64,256]{3,2,1,0:T(8,128)(2,1)S(1)}, bf16[1,4,64,256]{3,2,1,0:T(8,128)(2,1)}, u32[]{:S(2)}) copy-start(bf16[1,4,64,256]{3,2,1,0:T(8,128)(2,1)} %field_hbm.1) | copy-start | bytes 393220
  5.3 0.9 %copy-start.2 = (bf16[1,4,64,256]{3,2,1,0:T(8,128)(2,1)S(1)}, bf16[1,4,64,256]{3,2,1,0:T(8,128)(2,1)}, u32[]{:S(2)}) copy-start(bf16[1,4,64,256]{3,2,1,0:T(8,128)(2,1)} %cot_hbm.1) | copy-start | bytes 393220

commit v2 on v1

v2 whole, which is shorter than its diff:
```python
import functools
import math

import jax
import jax.numpy as jnp
from jax import lax
from jax.experimental import pallas as pl
from jax.experimental.pallas import tpu as pltpu
from jax.sharding import PartitionSpec as P

MESH = pl.DeviceIdType.MESH
F32 = jnp.float32
BF16 = jnp.bfloat16


FIRST_KEEPER = 10


def kernel_body(sizes, coeff_ref, field_hbm, cot_hbm, weight_hbm, out_v, gin_v, final,
                win, edge, cwin, cedge, cot, weight, fband, bband, conv, cot_t, a_send, a_recv,
                b_send, b_recv, c_send, local_sem, halo_send, halo_recv, a_ssem, a_rsem, b_ssem,
                b_rsem, c_ssem, c_rsem, near_sem, dp_sem):
    nz, nlon, ndp, basis, rows, cols, chans, taps = sizes
    reach = taps // 2
    nq = nlon // 2
    blk = chans // nlon
    scale = 1.0 / math.sqrt(ndp * nz * rows * nlon * cols)
    z = lax.axis_index("lat")
    lon = lax.axis_index("lon")
    dp = lax.axis_index("dp")
    q = lon // 2
    core = lon % 2
    mate = q * 2 + 1 - core
    block = cols + 2 * reach
    side = 2 * reach
    half = chans // ndp
    plane = nq * ndp

    def device(zz, ll, dd):
        return {"lat": zz, "lon": ll, "dp": dd}

    barrier = pltpu.get_barrier_semaphore()
    greeted = []

    def greet(*place):
        pl.semaphore_signal(barrier, inc=1, device_id=device(*place), device_id_type=MESH)
        greeted.append(place)

    up = lax.rem(z + 1, nz)
    down = lax.rem(z + nz - 1, nz)
    q_next = lax.rem(q + 1, nq)
    q_prev = lax.rem(q + nq - 1, nq)
    g = dp * nq + q
    for zz in (down, up):
        for cc in range(2):
            greet(zz, q * 2 + cc, dp)
    for zz in (down, up, z):
        greet(zz, q_prev * 2 + 1, dp)
        greet(zz, q_next * 2, dp)
    greet(z, mate, dp)
    for r in range(1, plane):
        place = lax.rem(g + r, plane)
        greet(z, lax.rem(place, nq) * 2 + core, place // nq)

    inside = (pl.ds(1, rows), pl.ds(side, cols))
    loads = [
        pltpu.make_async_copy(field_hbm.at[0], win.at[core, inside[0], inside[1]], local_sem.at[0]),
        pltpu.make_async_copy(cot_hbm.at[0], cot.at[core], local_sem.at[1]),
        pltpu.make_async_copy(cot_hbm.at[0], cwin.at[inside[0], inside[1]], local_sem.at[2]),
        pltpu.make_async_copy(weight_hbm, weight, local_sem.at[3]),
    ]
    for load in loads:
        load.start()

    pl.semaphore_wait(barrier, len(greeted))

    far = lax.rem(q + nq - 1 + 2 * core, nq)
    edge_cols = pl.ds(pl.multiple_of(core * (cols - side), 16), side)
    near_cols = pl.ds(pl.multiple_of((1 - core) * (cols - side), 16), side)
    started = []

    def send(src, dst, slots, zz, ll):
        copy = pltpu.make_async_remote_copy(
            src_ref=src, dst_ref=dst, send_sem=halo_send.at[slots[0]],
            recv_sem=halo_recv.at[slots[1]], device_id=device(zz, ll, dp), device_id_type=MESH)
        copy.start()
        started.append(copy)

    lat_sides = ((up, rows - 1, 0, 0), (down, 0, rows + 1, 1))
    for zz, row, place, which in lat_sides:
        for cc in range(2):
            send(field_hbm.at[0, row], win.at[core, place, inside[1]],
                 (which * 2 + cc, which * 2 + core), zz, q * 2 + cc)
    for zz, row, place, which in lat_sides:
        for cc in range(2):
            send(field_hbm.at[0, row, edge_cols], edge.at[1 - core, place],
                 (6 + which * 2 + cc, 6 + which * 2 + 1 - core), zz, far * 2 + cc)
    for cc in range(2):
        send(field_hbm.at[0, :, edge_cols], edge.at[1 - core, inside[0]],
             (4 + cc, 4 + 1 - core), z, far * 2 + cc)
    send(field_hbm.at[0], win.at[core, inside[0], inside[1]], (10, 10), z, mate)
    send(cot_hbm.at[0], cot.at[core], (11, 11), z, mate)
    for zz, row, place, which in lat_sides:
        send(cot_hbm.at[0, row], cwin.at[place, inside[1]], (12 + which, 12 + which), zz, lon)
        send(cot_hbm.at[0, row, near_cols], cedge.at[core, place], (14 + which, 14 + which),
             zz, mate)
        send(cot_hbm.at[0, row, edge_cols], cedge.at[1 - core, place], (16 + which, 16 + which),
             zz, far * 2 + 1 - core)
    send(cot_hbm.at[0, :, edge_cols], cedge.at[1 - core, inside[0]], (18, 18),
         z, far * 2 + 1 - core)

    def arrived(slot, like):
        pltpu.make_async_copy(like, like, halo_recv.at[slot]).wait()

    spans = []
    while 2 ** (len(spans) + 1) <= nz // 2:
        spans.append(2 ** len(spans))

    def tell(n):
        for way, step in ((0, spans[n]), (1, nz - spans[n])):
            pl.semaphore_signal(near_sem.at[n, way], inc=1,
                                device_id=device(lax.rem(z + step, nz), lon, dp),
                                device_id_type=MESH)

    def told(n):
        for way in range(2):
            pl.semaphore_wait(near_sem.at[n, way], 1)

    def relay(n):
        if 0 < n <= len(spans):
            told(n - 1)
        if n < len(spans):
            tell(n)

    relay(0)

    lanes = 3 * block + side
    tap_lane = lax.broadcasted_iota(jnp.int32, (128, lanes), 0)
    out_lane = lax.broadcasted_iota(jnp.int32, (128, lanes), 1)

    def make_band(dst, transposed):
        rowvec = jnp.zeros((rows * 16, lanes), F32)
        for a in range(3):
            if transposed:
                picked = coeff_ref[2 - a, pl.ds(16 * a, rows * 16), :]
                hit = (out_lane == reach + block * a + (taps - 1) - tap_lane) & (tap_lane < taps)
            else:
                picked = coeff_ref[a, pl.ds(16, rows * 16), :]
                hit = (out_lane == reach + block * a + tap_lane) & (tap_lane < taps)
            rowvec = rowvec + jnp.dot(picked, jnp.where(hit, 1.0, 0.0).astype(BF16),
                                      preferred_element_type=F32)
        for i in range(rows):
            for k in range(basis):
                row = jnp.broadcast_to(rowvec[i * 16 + k:i * 16 + k + 1, :], (cols, lanes))
                dst[i, pl.ds(k * cols, cols), :] = pltpu.roll(
                    row, 0, 1, stride=1, stride_axis=0).astype(BF16)

    make_band(fband, False)
    relay(1)

    for load in loads:
        load.wait()
    arrived(11, cot.at[0])
    for s in range(2):
        for i in range(0, rows, 2):
            pair = cot[s, pl.ds(i, 2)].reshape(2 * cols, chans).astype(F32)
            cot_t[:, :, :, pl.ds((s * rows + i) * cols, 2 * cols)] = pair.T.astype(
                BF16).reshape(nq, 2, blk, 2 * cols)

    for slot in range(4):
        arrived(slot, win.at[0, 0, inside[1]])
    for slot in range(4, 6):
        arrived(slot, edge.at[0, inside[0]])
    for slot in range(6, 10):
        arrived(slot, edge.at[0, 0])
    arrived(10, win.at[0, inside[0], inside[1]])

    def blank_field(place):
        for s in range(2):
            win[s, place, inside[1], :] = jnp.zeros((cols, chans), BF16)
            edge[s, place] = jnp.zeros((side, chans), BF16)

    @pl.when(z == 0)
    def _():
        blank_field(0)

    @pl.when(z == nz - 1)
    def _():
        blank_field(rows + 1)

    first_half = lax.broadcasted_iota(jnp.int32, (side, chans), 0) < reach
    nothing = jnp.zeros((side, chans), F32)

    def joint(before, after):
        before = nothing if before is None else before.astype(F32)
        after = nothing if after is None else after.astype(F32)
        return jnp.where(first_half, before, after).astype(BF16)

    for r in range(rows + 3):
        first, last = r == 0, r == rows + 2
        win[0, r, pl.ds(0, side), :] = joint(
            None if first else win[1, r - 1, pl.ds(side, side), :],
            None if last else edge[0, r])
        win[1, r, pl.ds(0, side), :] = joint(
            None if first else edge[1, r - 1],
            None if last else win[0, r, pl.ds(cols, side), :])

    for s in range(2):
        for i in range(rows):
            wide = jnp.concatenate([win[s, i], win[s, i + 1], win[s, i + 2],
                                    win[s, i + 3, pl.ds(0, side), :]], axis=0)
            part = jnp.dot(fband[i], wide, preferred_element_type=F32)
            conv[:, s * rows + i] = part.astype(BF16).reshape(basis, cols, chans)
    relay(2)

    mine_t = cot_t[:, core].reshape(nq * blk, 2 * rows * cols)
    for k in range(basis):
        terms = jnp.dot(mine_t, conv[k].reshape(2 * rows * cols, chans), preferred_element_type=F32)
        terms = terms.astype(BF16).reshape(nq, blk, chans)
        for h in range(ndp):
            a_send[h, :, k] = terms[:, :, h * half:(h + 1) * half]

    a_copies = []
    for r in range(1, plane):
        place = lax.rem(g + r, plane)
        to_q = lax.rem(place, nq)
        copy = pltpu.make_async_remote_copy(
            src_ref=a_send.at[place // nq, to_q], dst_ref=a_recv.at[r - 1],
            send_sem=a_ssem.at[r - 1], recv_sem=a_rsem.at[r - 1],
            device_id=device(z, to_q * 2 + core, place // nq), device_id_type=MESH)
        copy.start()
        a_copies.append(copy)

    make_band(bband, True)
    total = jnp.zeros((rows * cols, chans), F32)
    for k in range(basis):
        own = conv[k, pl.ds(core * rows, rows)].reshape(rows * cols, chans)
        total = total + jnp.dot(own, weight[k], preferred_element_type=F32)
    out_v[0] = total.astype(BF16).reshape(rows, cols, chans)

    for slot in range(12, 14):
        arrived(slot, cwin.at[0, inside[1]])
    for slot in range(14, 18):
        arrived(slot, cedge.at[0, 0])
    arrived(18, cedge.at[0, inside[0]])
    cedge[1 - core, inside[0]] = cot[1 - core, :, edge_cols, :]

    def blank_cot(place):
        cwin[place, inside[1], :] = jnp.zeros((cols, chans), BF16)
        for s in range(2):
            cedge[s, place] = jnp.zeros((side, chans), BF16)

    @pl.when(z == 0)
    def _():
        blank_cot(0)

    @pl.when(z == nz - 1)
    def _():
        blank_cot(rows + 1)

    for r in range(rows + 3):
        cwin[r, pl.ds(0, side), :] = joint(
            None if r == 0 else cedge[1, r - 1], None if r == rows + 2 else cedge[0, r])
    for i in range(rows):
        wide = jnp.concatenate(
            [cwin[i], cwin[i + 1], cwin[i + 2], cwin[i + 3, pl.ds(0, side), :]], axis=0)
        part = jnp.dot(bband[i], wide, preferred_element_type=F32)
        conv[:, i] = part.astype(BF16).reshape(basis, cols, chans)
    total = jnp.zeros((rows * cols, chans), F32)
    for k in range(basis):
        own = conv[k, pl.ds(0, rows)].reshape(rows * cols, chans)
        total = total + lax.dot_general(own, weight[k], (((1,), (1,)), ((), ())),
                                        preferred_element_type=F32)
    gin_v[0] = total.astype(BF16).reshape(rows, cols, chans)
    relay(3)
    pl.semaphore_signal(dp_sem, inc=1, device_id=device(z, lon, 1 - dp), device_id_type=MESH)

    for copy in a_copies:
        copy.wait_recv()
    for k in range(basis):
        summed = a_send[dp, q, k].astype(F32)
        for r in range(plane - 1):
            summed = summed + a_recv[r, k].astype(F32)
        b_send[k] = summed.astype(BF16)

    def keeper(k):
        return (FIRST_KEEPER + k) % nz

    for k in range(basis):
        @pl.when(z != keeper(k))
        def _(k=k):
            pltpu.make_async_remote_copy(
                src_ref=b_send.at[k], dst_ref=b_recv.at[z], send_sem=b_ssem.at[k],
                recv_sem=b_rsem.at[z], device_id=device(keeper(k), lon, dp),
                device_id_type=MESH).start()

    my_k = lax.rem(z + nz - FIRST_KEEPER % nz, nz)
    keeps = my_k < basis
    my_k = jnp.minimum(my_k, basis - 1)
    my_lanes = pl.ds(pl.multiple_of(dp * half, half), half)
    pl.semaphore_wait(dp_sem, 1)

    @pl.when(keeps)
    def _():
        for r in range(1, nz):
            place = lax.rem(z + r, nz)
            pltpu.make_async_copy(b_recv.at[place], b_recv.at[place], b_rsem.at[place]).wait()
        b_recv[z] = b_send[my_k]
        summed = jnp.zeros((blk, half), F32)
        for r in range(nz):
            summed = summed + b_recv[r].astype(F32)
        c_send[...] = (summed * scale).astype(BF16)
        for zz in range(nz):
            for dd in range(ndp):
                @pl.when(jnp.logical_or(z != zz, dp != dd))
                def _(zz=zz, dd=dd):
                    pltpu.make_async_remote_copy(
                        src_ref=c_send, dst_ref=final.at[my_k, :, my_lanes],
                        send_sem=c_ssem.at[dd * nz + zz], recv_sem=c_rsem.at[my_k * ndp + dp],
                        device_id=device(zz, lon, dd), device_id_type=MESH).start()
        final[my_k, :, my_lanes] = c_send[...]

    for k in range(basis):
        for h in range(ndp):
            @pl.when(jnp.logical_or(z != keeper(k), dp != h))
            def _(k=k, h=h):
                spot = final.at[k, :, pl.ds(h * half, half)]
                pltpu.make_async_copy(spot, spot, c_rsem.at[k * ndp + h]).wait()

    for copy in started:
        copy.wait_send()
    for copy in a_copies:
        copy.wait_send()
    for k in range(basis):
        @pl.when(z != keeper(k))
        def _(k=k):
            pltpu.make_async_copy(b_send.at[k], b_send.at[k], b_ssem.at[k]).wait()

    @pl.when(keeps)
    def _():
        for zz in range(nz):
            for dd in range(ndp):
                @pl.when(jnp.logical_or(z != zz, dp != dd))
                def _(zz=zz, dd=dd):
                    pltpu.make_async_copy(c_send, c_send, c_ssem.at[dd * nz + zz]).wait()


def hand_over(*refs):
    count = (len(refs) - 1) // 2
    copies = [pltpu.make_async_copy(refs[n], refs[count + n], refs[-1].at[n]) for n in range(count)]
    for copy in copies:
        copy.start()
    for copy in copies:
        copy.wait()


def on_device(input_field, cotangent, channel_weight, basis_filter, reach_cols):
    _, rows, cols, chans = input_field.shape
    basis, nlat, spans, taps = basis_filter.shape
    reach = taps // 2
    nz, nlon, ndp = (lax.axis_size(name) for name in ("lat", "lon", "dp"))
    nq = nlon // 2
    blk = chans // nlon
    block = cols + 2 * reach
    side = 2 * reach
    lanes = spans * block + side
    half = chans // ndp
    plane = nq * ndp

    first = lax.axis_index("lat") * rows
    offsets = jnp.abs(jnp.arange(taps, dtype=jnp.int32) - reach)
    inside = offsets[None, :] <= reach_cols[:, None]
    masked = jnp.where(inside[None, :, None, :], basis_filter, 0)
    near = lax.dynamic_slice_in_dim(jnp.pad(masked, ((0, 0), (1, 1), (0, 0), (0, 0))),
                                    first, rows + 2, 1)
    coeff = jnp.transpose(near, (2, 1, 0, 3))
    coeff = jnp.pad(coeff, ((0, 0), (0, 0), (0, 16 - basis), (0, 128 - taps)))
    coeff = coeff.reshape(spans, (rows + 2) * 16, 128).astype(BF16)

    sizes = (nz, nlon, ndp, basis, rows, cols, chans, taps)
    vmem = pl.BlockSpec(memory_space=pltpu.VMEM)
    hbm = pl.BlockSpec(memory_space=pltpu.HBM)
    dma = pltpu.SemaphoreType.DMA
    shapes = (jax.ShapeDtypeStruct(input_field.shape, BF16),
              jax.ShapeDtypeStruct(input_field.shape, BF16),
              jax.ShapeDtypeStruct((basis, blk, chans), BF16))
    results = pl.pallas_call(
        functools.partial(kernel_body, sizes),
        out_shape=shapes,
        in_specs=[vmem, hbm, hbm, hbm],
        out_specs=(vmem, vmem, vmem),
        scratch_shapes=[
            pltpu.VMEM((2, rows + 3, block, chans), BF16),
            pltpu.VMEM((2, rows + 2, side, chans), BF16),
            pltpu.VMEM((rows + 3, block, chans), BF16),
            pltpu.VMEM((2, rows + 2, side, chans), BF16),
            pltpu.VMEM((2, rows, cols, chans), BF16),
            pltpu.VMEM((basis, chans, chans), BF16),
            pltpu.VMEM((rows, basis * cols, lanes), BF16),
            pltpu.VMEM((rows, basis * cols, lanes), BF16),
            pltpu.VMEM((basis, 2 * rows, cols, chans), BF16),
            pltpu.VMEM((nq, 2, blk, 2 * rows * cols), BF16),
            pltpu.VMEM((ndp, nq, basis, blk, half), BF16),
            pltpu.VMEM((plane - 1, basis, blk, half), BF16),
            pltpu.VMEM((basis, blk, half), BF16),
            pltpu.VMEM((nz, blk, half), BF16),
            pltpu.VMEM((blk, half), BF16),
            dma((4,)), dma((19,)), dma((19,)), dma((plane - 1,)), dma((plane - 1,)),
            dma((basis,)), dma((nz,)), dma((nz * ndp,)), dma((basis * ndp,)),
            pltpu.SemaphoreType.REGULAR((4, 2)), pltpu.SemaphoreType.REGULAR,
        ],
        compiler_params=pltpu.CompilerParams(
            collective_id=0, has_side_effects=True),
        name="disco_block",
    )(coeff, input_field, cotangent, channel_weight)
    anywhere = pl.BlockSpec(memory_space=pl.ANY)
    out, gin, gw = pl.pallas_call(
        hand_over,
        out_shape=shapes,
        in_specs=[vmem] * 3,
        out_specs=(hbm, hbm, hbm),
        scratch_shapes=[dma((3,))],
        name="hand_over",
    )(*results)
    return out, gin, jnp.transpose(gw, (0, 2, 1))


def solution(mesh):
    placed = (P("dp", "lat", "lon", None), P("dp", "lat", "lon", None), P(), P(), P())
    return jax.shard_map(
        on_device,
        mesh=mesh,
        in_specs=placed,
        out_specs=(P("dp", "lat", "lon", None), P("dp", "lat", "lon", None), P(None, None, "lon")),
        check_vma=False,
    )
```

time: 63 us -> 54 us (0.86)
  the two profiles are of different devices: /device:TPU:8 before, /device:TPU:1 now
where the time goes in v2:
time: 54 us; the launch traced here: 53.8 us
  Pallas kernels  50 us (93%)
  other arithmetic  1.73 us (3%)
  local copies, waits for them, and re-layouts  1.37 us (3%)
  between operations  0.66 us (1%)
    pallas_call x1, Pallas kernels, on_device(): pl.pallas_call(functools.partial(kernel_body, sizes), out_shape=shapes, i...  48.3 us
    pallas_call x1, Pallas kernels, on_device(): pl.pallas_call(hand_over, out_shape=shapes, in_specs=[vmem] * 3, out_spec...  1.76 us

profile of v2, /device:TPU:1, one launch (start us, length us, event | category | flops | bytes accessed | tf_op | source)
XLA Modules:
  0.0 53.8 jit_solution(10623730391363278963)
XLA Ops:
  0.6 0.7 %broadcast_compare_fusion = pred[64,17]{0,1:T(8,128)(4,1)S(1)} fusion(s32[64]{0:T(128)} %param.9, s32[17]{0:T(128)S(1)} %add_abs_fusion), kind=kLoop, calls=%fused_computation.2 | loop fusion | flops 1088 | bytes 1412 | tf_op jit(solution)/shard_map/le | solution.py:372
  1.4 1.0 %broadcast_select_fusion = bf16[9,64,3,17]{1,2,3,0:T(4,128)(2,1)S(1)} fusion(bf16[9,64,3,17]{1,2,3,0:T(4,128)(2,1)} %param.8, pred[64,17]{0,1:T(8,128)(4,1)S(1)} %broadcast_compare_fusion), kind=kLoop, calls=%fused_computation.1 | loop fusion | flops 29376 | bytes 118592 | tf_op jit(solution)/shard_map/jit(_where)/select_n | solution.py:373
  2.4 0.3 dynamic-slice_bitcast_fusion
  2.6 0.4 copy.9
  3.1 0.7 %pad.9.clone = bf16[3,6,16,128]{3,2,1,0:T(8,128)(2,1)} pad(bf16[3,6,9,17]{3,2,1,0:T(8,128)(2,1)S(1)} %copy.9, bf16[]{:T(256)} %constant.5.clone.1), padding=0_0x0_0x0_7x0_111 | pad | bytes 79238 | tf_op jit(solution)/shard_map/jit(_pad)/pad | solution.py:377
  3.8 48.3 %disco_block.1 = (bf16[1,4,64,256]{3,2,1,0:T(8,128)(2,1)}, bf16[1,4,64,256]{3,2,1,0:T(8,128)(2,1)}, bf16[9,16,256]{2,1,0:T(8,128)(2,1)}) custom-call(bf16[3,96,128]{2,1,0:T(8,128)(2,1)} %bitcast.4, bf16[1,4,64,256]{3,2,1,0:T(8,128)(2,1)} %field_hbm.1, bf16[1,4,64,256]{3,2,1,0:T(8,128)(2,1)} %cot_hbm.1, bf16[9,256,256]{2,1,0:T(8,128)(2,1)} %weight_hbm.1), custom_call_target="tpu_custom_call" | custom-call | tf_op jit(solution)/shard_map/disco_block/pallas_call | solution.py:387
  52.0 1.8 %hand_over.1 = (bf16[1,4,64,256]{3,2,1,0:T(8,128)(2,1)}, bf16[1,4,64,256]{3,2,1,0:T(8,128)(2,1)}, bf16[9,16,256]{2,1,0:T(8,128)(2,1)}) custom-call(bf16[1,4,64,256]{3,2,1,0:T(8,128)(2,1)} %get-tuple-element.9.refs_0_, bf16[1,4,64,256]{3,2,1,0:T(8,128)(2,1)} %get-tuple-element.10.refs_1_, bf16[9,16,256]{2,1,0:T(8,128)(2,1)} %get-tuple-element.11.refs_2_), custom_call_target="tpu_custom_call" | custom-call | tf_op jit(solution)/shard_map/hand_over/pallas_call | solution.py:417
  (1 shorter events, 0.0 us)

commit v3 on v2

--- a/solution.py
+++ b/solution.py
@@ -13,14 +13,15 @@
 BF16 = jnp.bfloat16
 
 
-FIRST_KEEPER = 10
-
-
-def kernel_body(sizes, coeff_ref, field_hbm, cot_hbm, weight_hbm, out_v, gin_v, final,
-                win, edge, cwin, cedge, cot, weight, fband, bband, conv, cot_t, a_send, a_recv,
+KEEPERS = (10, 11, 2, 12, 13, 1, 14, 15, 0)
+GROUP = 3
+
+
+def kernel_body(sizes, coeff_hbm, reach_hbm, field_hbm, cot_hbm, weight_hbm, out_hbm, gin_hbm,
+                gw_hbm, coeff, reach_cols, out_v, gin_v, final, win, edge, cwin, cedge, cot, weight, fband, bband, conv, cot_t, a_send, a_recv,
                 b_send, b_recv, c_send, local_sem, halo_send, halo_recv, a_ssem, a_rsem, b_ssem,
                 b_rsem, c_ssem, c_rsem, near_sem, dp_sem):
-    nz, nlon, ndp, basis, rows, cols, chans, taps = sizes
+    nz, nlon, ndp, nlat, basis, rows, cols, chans, taps = sizes
     reach = taps // 2
     nq = nlon // 2
     blk = chans // nlon
@@ -69,7 +70,11 @@
         pltpu.make_async_copy(cot_hbm.at[0], cwin.at[inside[0], inside[1]], local_sem.at[2]),
         pltpu.make_async_copy(weight_hbm, weight, local_sem.at[3]),
     ]
-    for load in loads:
+    small_loads = [
+        pltpu.make_async_copy(coeff_hbm, coeff, local_sem.at[4]),
+        pltpu.make_async_copy(reach_hbm, reach_cols, local_sem.at[5]),
+    ]
+    for load in small_loads + loads:
         load.start()
 
     pl.semaphore_wait(barrier, len(greeted))
@@ -135,28 +140,35 @@
     relay(0)
 
     lanes = 3 * block + side
-    tap_lane = lax.broadcasted_iota(jnp.int32, (128, lanes), 0)
-    out_lane = lax.broadcasted_iota(jnp.int32, (128, lanes), 1)
+    tap_lane = lax.broadcasted_iota(jnp.int32, (taps, lanes), 0)
+    out_lane = lax.broadcasted_iota(jnp.int32, (taps, lanes), 1)
+    distance = jnp.abs(lax.broadcasted_iota(jnp.int32, (basis, taps), 1) - reach)
+    first_row = z * rows
+    held_row = jnp.clip(first_row - 1, 0, nlat - (rows + 2))
 
     def make_band(dst, transposed):
-        rowvec = jnp.zeros((rows * 16, lanes), F32)
-        for a in range(3):
-            if transposed:
-                picked = coeff_ref[2 - a, pl.ds(16 * a, rows * 16), :]
-                hit = (out_lane == reach + block * a + (taps - 1) - tap_lane) & (tap_lane < taps)
-            else:
-                picked = coeff_ref[a, pl.ds(16, rows * 16), :]
-                hit = (out_lane == reach + block * a + tap_lane) & (tap_lane < taps)
-            rowvec = rowvec + jnp.dot(picked, jnp.where(hit, 1.0, 0.0).astype(BF16),
-                                      preferred_element_type=F32)
         for i in range(rows):
+            rowvec = jnp.zeros((basis, lanes), F32)
+            for a in range(3):
+                if transposed:
+                    row = jnp.clip(first_row + i - 1 + a, 0, nlat - 1)
+                    picked = coeff[2 - a, row - held_row]
+                    hit = out_lane == reach + block * a + (taps - 1) - tap_lane
+                else:
+                    row = first_row + i
+                    picked = coeff[a, row - held_row]
+                    hit = out_lane == reach + block * a + tap_lane
+                picked = jnp.where(distance <= reach_cols[row], picked.astype(F32), 0.0)
+                rowvec = rowvec + jnp.dot(picked.astype(BF16), jnp.where(hit, 1.0, 0.0).astype(BF16),
+                                          preferred_element_type=F32)
             for k in range(basis):
-                row = jnp.broadcast_to(rowvec[i * 16 + k:i * 16 + k + 1, :], (cols, lanes))
+                wide = jnp.broadcast_to(rowvec[k:k + 1, :], (cols, lanes))
                 dst[i, pl.ds(k * cols, cols), :] = pltpu.roll(
-                    row, 0, 1, stride=1, stride_axis=0).astype(BF16)
-
+                    wide, 0, 1, stride=1, stride_axis=0).astype(BF16)
+
+    for load in small_loads:
+        load.wait()
     make_band(fband, False)
-    relay(1)
 
     for load in loads:
         load.wait()
@@ -174,6 +186,7 @@
     for slot in range(6, 10):
         arrived(slot, edge.at[0, 0])
     arrived(10, win.at[0, inside[0], inside[1]])
+    relay(1)
 
     def blank_field(place):
         for s in range(2):
@@ -211,32 +224,39 @@
                                     win[s, i + 3, pl.ds(0, side), :]], axis=0)
             part = jnp.dot(fband[i], wide, preferred_element_type=F32)
             conv[:, s * rows + i] = part.astype(BF16).reshape(basis, cols, chans)
+
+    mine_t = cot_t[:, core].reshape(nq * blk, 2 * rows * cols)
+    groups = [range(n, min(n + GROUP, basis)) for n in range(0, basis, GROUP)]
+    a_copies = []
+    for n, group in enumerate(groups):
+        for k in group:
+            terms = jnp.dot(mine_t, conv[k].reshape(2 * rows * cols, chans),
+                            preferred_element_type=F32)
+            terms = terms.astype(BF16).reshape(nq, blk, chans)
+            for h in range(ndp):
+                a_send[h, :, k] = terms[:, :, h * half:(h + 1) * half]
+        part = pl.ds(group[0], len(group))
+        copies = []
+        for r in range(1, plane):
+            place = lax.rem(g + r, plane)
+            to_q = lax.rem(place, nq)
+            copy = pltpu.make_async_remote_copy(
+                src_ref=a_send.at[place // nq, to_q, part], dst_ref=a_recv.at[r - 1, part],
+                send_sem=a_ssem.at[n, r - 1], recv_sem=a_rsem.at[n, r - 1],
+                device_id=device(z, to_q * 2 + core, place // nq), device_id_type=MESH)
+            copy.start()
+            copies.append(copy)
+        a_copies.append(copies)
     relay(2)
-
-    mine_t = cot_t[:, core].reshape(nq * blk, 2 * rows * cols)
-    for k in range(basis):
-        terms = jnp.dot(mine_t, conv[k].reshape(2 * rows * cols, chans), preferred_element_type=F32)
-        terms = terms.astype(BF16).reshape(nq, blk, chans)
-        for h in range(ndp):
-            a_send[h, :, k] = terms[:, :, h * half:(h + 1) * half]
-
-    a_copies = []
-    for r in range(1, plane):
-        place = lax.rem(g + r, plane)
-        to_q = lax.rem(place, nq)
-        copy = pltpu.make_async_remote_copy(
-            src_ref=a_send.at[place // nq, to_q], dst_ref=a_recv.at[r - 1],
-            send_sem=a_ssem.at[r - 1], recv_sem=a_rsem.at[r - 1],
-            device_id=device(z, to_q * 2 + core, place // nq), device_id_type=MESH)
-        copy.start()
-        a_copies.append(copy)
 
     make_band(bband, True)
     total = jnp.zeros((rows * cols, chans), F32)
     for k in range(basis):
         own = conv[k, pl.ds(core * rows, rows)].reshape(rows * cols, chans)
         total = total + jnp.dot(own, weight[k], preferred_element_type=F32)
-    out_v[0] = total.astype(BF16).reshape(rows, cols, chans)
+    out_v[...] = total.astype(BF16).reshape(rows, cols, chans)
+    out_copy = pltpu.make_async_copy(out_v, out_hbm.at[0], local_sem.at[0])
+    out_copy.start()
 
     for slot in range(12, 14):
         arrived(slot, cwin.at[0, inside[1]])
@@ -271,30 +291,34 @@
         own = conv[k, pl.ds(0, rows)].reshape(rows * cols, chans)
         total = total + lax.dot_general(own, weight[k], (((1,), (1,)), ((), ())),
                                         preferred_element_type=F32)
-    gin_v[0] = total.astype(BF16).reshape(rows, cols, chans)
+    gin_v[...] = total.astype(BF16).reshape(rows, cols, chans)
+    gin_copy = pltpu.make_async_copy(gin_v, gin_hbm.at[0], local_sem.at[1])
+    gin_copy.start()
     relay(3)
     pl.semaphore_signal(dp_sem, inc=1, device_id=device(z, lon, 1 - dp), device_id_type=MESH)
 
-    for copy in a_copies:
-        copy.wait_recv()
+    def keeper(k):
+        return KEEPERS[k] % nz
+
+    for n, group in enumerate(groups):
+        for copy in a_copies[n]:
+            copy.wait_recv()
+        for k in group:
+            summed = a_send[dp, q, k].astype(F32)
+            for r in range(plane - 1):
+                summed = summed + a_recv[r, k].astype(F32)
+            b_send[k] = summed.astype(BF16)
+
+            @pl.when(z != keeper(k))
+            def _(k=k):
+                pltpu.make_async_remote_copy(
+                    src_ref=b_send.at[k], dst_ref=b_recv.at[z], send_sem=b_ssem.at[k],
+                    recv_sem=b_rsem.at[z], device_id=device(keeper(k), lon, dp),
+                    device_id_type=MESH).start()
+
+    my_k = jnp.int32(basis)
     for k in range(basis):
-        summed = a_send[dp, q, k].astype(F32)
-        for r in range(plane - 1):
-            summed = summed + a_recv[r, k].astype(F32)
-        b_send[k] = summed.astype(BF16)
-
-    def keeper(k):
-        return (FIRST_KEEPER + k) % nz
-
-    for k in range(basis):
-        @pl.when(z != keeper(k))
-        def _(k=k):
-            pltpu.make_async_remote_copy(
-                src_ref=b_send.at[k], dst_ref=b_recv.at[z], send_sem=b_ssem.at[k],
-                recv_sem=b_rsem.at[z], device_id=device(keeper(k), lon, dp),
-                device_id_type=MESH).start()
-
-    my_k = lax.rem(z + nz - FIRST_KEEPER % nz, nz)
+        my_k = jnp.where(z == keeper(k), k, my_k)
     keeps = my_k < basis
     my_k = jnp.minimum(my_k, basis - 1)
     my_lanes = pl.ds(pl.multiple_of(dp * half, half), half)
@@ -310,7 +334,7 @@
         for r in range(nz):
             summed = summed + b_recv[r].astype(F32)
         c_send[...] = (summed * scale).astype(BF16)
-        for zz in range(nz):
+        for zz in sorted(range(nz), key=lambda zz: (zz + nz // 2 + 1) % nz, reverse=True):
             for dd in range(ndp):
                 @pl.when(jnp.logical_or(z != zz, dp != dd))
                 def _(zz=zz, dd=dd):
@@ -327,10 +351,14 @@
                 spot = final.at[k, :, pl.ds(h * half, half)]
                 pltpu.make_async_copy(spot, spot, c_rsem.at[k * ndp + h]).wait()
 
+    gw_copy = pltpu.make_async_copy(final, gw_hbm, local_sem.at[2])
+    gw_copy.start()
+
     for copy in started:
         copy.wait_send()
-    for copy in a_copies:
-        copy.wait_send()
+    for copies in a_copies:
+        for copy in copies:
+            copy.wait_send()
     for k in range(basis):
         @pl.when(z != keeper(k))
         def _(k=k):
@@ -343,6 +371,10 @@
                 @pl.when(jnp.logical_or(z != zz, dp != dd))
                 def _(zz=zz, dd=dd):
                     pltpu.make_async_copy(c_send, c_send, c_ssem.at[dd * nz + zz]).wait()
+
+    out_copy.wait()
+    gin_copy.wait()
+    gw_copy.wait()
 
 
 def hand_over(*refs):
@@ -358,6 +390,7 @@
     _, rows, cols, chans = input_field.shape
     basis, nlat, spans, taps = basis_filter.shape
     reach = taps // 2
+    groups = pl.cdiv(basis, GROUP)
     nz, nlon, ndp = (lax.axis_size(name) for name in ("lat", "lon", "dp"))
     nq = nlon // 2
     blk = chans // nlon
@@ -368,16 +401,9 @@
     plane = nq * ndp
 
     first = lax.axis_index("lat") * rows
-    offsets = jnp.abs(jnp.arange(taps, dtype=jnp.int32) - reach)
-    inside = offsets[None, :] <= reach_cols[:, None]
-    masked = jnp.where(inside[None, :, None, :], basis_filter, 0)
-    near = lax.dynamic_slice_in_dim(jnp.pad(masked, ((0, 0), (1, 1), (0, 0), (0, 0))),
-                                    first, rows + 2, 1)
-    coeff = jnp.transpose(near, (2, 1, 0, 3))
-    coeff = jnp.pad(coeff, ((0, 0), (0, 0), (0, 16 - basis), (0, 128 - taps)))
-    coeff = coeff.reshape(spans, (rows + 2) * 16, 128).astype(BF16)
-
-    sizes = (nz, nlon, ndp, basis, rows, cols, chans, taps)
+    start = jnp.clip(first - 1, 0, nlat - (rows + 2))
+    coeff = jnp.transpose(lax.dynamic_slice_in_dim(basis_filter, start, rows + 2, 1), (2, 1, 0, 3))
+    sizes = (nz, nlon, ndp, nlat, basis, rows, cols, chans, taps)
     vmem = pl.BlockSpec(memory_space=pltpu.VMEM)
     hbm = pl.BlockSpec(memory_space=pltpu.HBM)
     dma = pltpu.SemaphoreType.DMA
@@ -387,9 +413,14 @@
     results = pl.pallas_call(
         functools.partial(kernel_body, sizes),
         out_shape=shapes,
-        in_specs=[vmem, hbm, hbm, hbm],
-        out_specs=(vmem, vmem, vmem),
+        in_specs=[hbm] * 5,
+        out_specs=(hbm, hbm, hbm),
         scratch_shapes=[
+            pltpu.VMEM((spans, rows + 2, basis, taps), BF16),
+            pltpu.SMEM((nlat,), jnp.int32),
+            pltpu.VMEM((rows, cols, chans), BF16),
+            pltpu.VMEM((rows, cols, chans), BF16),
+            pltpu.VMEM((basis, blk, chans), BF16),
             pltpu.VMEM((2, rows + 3, block, chans), BF16),
             pltpu.VMEM((2, rows + 2, side, chans), BF16),
             pltpu.VMEM((rows + 3, block, chans), BF16),
@@ -405,14 +436,14 @@
             pltpu.VMEM((basis, blk, half), BF16),
             pltpu.VMEM((nz, blk, half), BF16),
             pltpu.VMEM((blk, half), BF16),
-            dma((4,)), dma((19,)), dma((19,)), dma((plane - 1,)), dma((plane - 1,)),
+            dma((6,)), dma((19,)), dma((19,)), dma((groups, plane - 1)), dma((groups, plane - 1)),
             dma((basis,)), dma((nz,)), dma((nz * ndp,)), dma((basis * ndp,)),
             pltpu.SemaphoreType.REGULAR((4, 2)), pltpu.SemaphoreType.REGULAR,
         ],
         compiler_params=pltpu.CompilerParams(
             collective_id=0, has_side_effects=True),
         name="disco_block",
-    )(coeff, input_field, cotangent, channel_weight)
+    )(coeff, reach_cols, input_field, cotangent, channel_weight)
     anywhere = pl.BlockSpec(memory_space=pl.ANY)
     out, gin, gw = pl.pallas_call(
         hand_over,

time: 54 us -> 51.5 us (0.954)
  other arithmetic: 1.73 us -> 0 us
  Pallas kernels: 50 us -> 48.5 us
  local copies, waits for them, and re-layouts: 1.37 us -> 2.14 us
    unnamed x1 -> x3, local copies, waits for them, and re-layouts: 0.44 us -> 1.99 us
    pallas_call x1, Pallas kernels: 48.3 us -> 46.8 us  [on_device(): pl.pallas_call(functools.partial(kernel_body, sizes), out_shape=shapes, i...]
    select_n x1 -> x0, other arithmetic: 0.99 us -> none  [on_device(): masked = jnp.where(inside[None, :, None, :], basis_filter, 0)]
    le x1 -> x0, other arithmetic: 0.73 us -> none  [on_device(): inside = offsets[None, :] <= reach_cols[:, None]]
    pad x1 -> x0, local copies, waits for them, and re-layouts: 0.67 us -> none  [on_device(): coeff = jnp.pad(coeff, ((0, 0), (0, 0), (0, 16 - basis), (0, 128 - taps)))]
where the time goes in v3:
time: 51.5 us; the launch traced here: 51.3 us
  Pallas kernels  48.5 us (94%)
  local copies, waits for them, and re-layouts  2.14 us (4%)
  between operations  0.66 us (1%)
    pallas_call x1, Pallas kernels, on_device(): pl.pallas_call(functools.partial(kernel_body, sizes), out_shape=shapes, i...  46.8 us
    unnamed x3, local copies, waits for them, and re-layouts  1.99 us
    pallas_call x1, Pallas kernels, on_device(): pl.pallas_call(hand_over, out_shape=shapes, in_specs=[vmem] * 3, out_spec...  1.76 us

profile of v3, /device:TPU:1, one launch (start us, length us, event | category | flops | bytes accessed | tf_op | source)
XLA Modules:
  0.0 51.3 jit_solution(5069414182573897487)
XLA Ops:
  0.6 0.0 copy-start
  0.7 0.9 %copy-done = bf16[9,64,3,17]{1,2,3,0:T(4,128)(2,1)S(1)} copy-done((bf16[9,64,3,17]{1,2,3,0:T(4,128)(2,1)S(1)}, bf16[9,64,3,17]{1,2,3,0:T(4,128)(2,1)}, u32[]{:S(2)}) %copy-start) | copy-done | bytes 58776
  1.5 0.2 constant_dynamic-slice_fusion
  1.7 1.1 %copy.9 = bf16[9,6,3,17]{3,0,1,2:T(8,128)(2,1)} copy(bf16[9,6,3,17]{1,2,3,0:T(4,128)(2,1)S(1)} %constant_dynamic-slice_fusion) | data formatting | bytes 11016
  2.8 46.8 %disco_block.1 = (bf16[1,4,64,256]{3,2,1,0:T(8,128)(2,1)}, bf16[1,4,64,256]{3,2,1,0:T(8,128)(2,1)}, bf16[9,16,256]{2,1,0:T(8,128)(2,1)}) custom-call(bf16[3,6,9,17]{3,2,1,0:T(8,128)(2,1)} %bitcast.2, s32[64]{0:T(128)} %reach_hbm.1, bf16[1,4,64,256]{3,2,1,0:T(8,128)(2,1)} %field_hbm.1, bf16[1,4,64,256]{3,2,1,0:T(8,128)(2,1)} %cot_hbm.1, ...), custom_call_target="tpu_custom_call" | custom-call | tf_op jit(solution)/shard_map/disco_block/pallas_call | solution.py:413
  49.6 1.8 %hand_over.1 = (bf16[1,4,64,256]{3,2,1,0:T(8,128)(2,1)}, bf16[1,4,64,256]{3,2,1,0:T(8,128)(2,1)}, bf16[9,16,256]{2,1,0:T(8,128)(2,1)}) custom-call(bf16[1,4,64,256]{3,2,1,0:T(8,128)(2,1)} %get-tuple-element.9.refs_0_, bf16[1,4,64,256]{3,2,1,0:T(8,128)(2,1)} %get-tuple-element.10.refs_1_, bf16[9,16,256]{2,1,0:T(8,128)(2,1)} %get-tuple-element.11.refs_2_), custom_call_target="tpu_custom_call" | custom-call | tf_op jit(solution)/shard_map/hand_over/pallas_call | solution.py:448
Async XLA Ops:
  0.6 0.9 %copy-start = (bf16[9,64,3,17]{1,2,3,0:T(4,128)(2,1)S(1)}, bf16[9,64,3,17]{1,2,3,0:T(4,128)(2,1)}, u32[]{:S(2)}) copy-start(bf16[9,64,3,17]{1,2,3,0:T(4,128)(2,1)} %param.8) | copy-start | bytes 176260

commit v4 on v3

--- a/solution.py
+++ b/solution.py
@@ -13,14 +13,15 @@
 BF16 = jnp.bfloat16
 
 
-KEEPERS = (10, 11, 2, 12, 13, 1, 14, 15, 0)
+KEEPERS = (12, 3, 11, 13, 2, 14, 15, 1, 0)
 GROUP = 3
 
 
 def kernel_body(sizes, coeff_hbm, reach_hbm, field_hbm, cot_hbm, weight_hbm, out_hbm, gin_hbm,
                 gw_hbm, coeff, reach_cols, out_v, gin_v, final, win, edge, cwin, cedge, cot, weight, fband, bband, conv, cot_t, a_send, a_recv,
                 b_send, b_recv, c_send, local_sem, halo_send, halo_recv, a_ssem, a_rsem, b_ssem,
-                b_rsem, c_ssem, c_rsem, near_sem, dp_sem):
+                b_rsem, c_ssem, c_rsem, near_sem, plane_sem,
+                dp_sem):
     nz, nlon, ndp, nlat, basis, rows, cols, chans, taps = sizes
     reach = taps // 2
     nq = nlon // 2
@@ -40,29 +41,6 @@
     def device(zz, ll, dd):
         return {"lat": zz, "lon": ll, "dp": dd}
 
-    barrier = pltpu.get_barrier_semaphore()
-    greeted = []
-
-    def greet(*place):
-        pl.semaphore_signal(barrier, inc=1, device_id=device(*place), device_id_type=MESH)
-        greeted.append(place)
-
-    up = lax.rem(z + 1, nz)
-    down = lax.rem(z + nz - 1, nz)
-    q_next = lax.rem(q + 1, nq)
-    q_prev = lax.rem(q + nq - 1, nq)
-    g = dp * nq + q
-    for zz in (down, up):
-        for cc in range(2):
-            greet(zz, q * 2 + cc, dp)
-    for zz in (down, up, z):
-        greet(zz, q_prev * 2 + 1, dp)
-        greet(zz, q_next * 2, dp)
-    greet(z, mate, dp)
-    for r in range(1, plane):
-        place = lax.rem(g + r, plane)
-        greet(z, lax.rem(place, nq) * 2 + core, place // nq)
-
     inside = (pl.ds(1, rows), pl.ds(side, cols))
     loads = [
         pltpu.make_async_copy(field_hbm.at[0], win.at[core, inside[0], inside[1]], local_sem.at[0]),
@@ -77,11 +55,45 @@
     for load in small_loads + loads:
         load.start()
 
+    barrier = pltpu.get_barrier_semaphore()
+    greeted = []
+
+    def greet(*place):
+        pl.semaphore_signal(barrier, inc=1, device_id=device(*place), device_id_type=MESH)
+        greeted.append(place)
+
+    up = lax.rem(z + 1, nz)
+    down = lax.rem(z + nz - 1, nz)
+    q_next = lax.rem(q + 1, nq)
+    q_prev = lax.rem(q + nq - 1, nq)
+    g = dp * nq + q
+    for zz in (down, up):
+        for cc in range(2):
+            greet(zz, q * 2 + cc, dp)
+    for zz in (down, up, z):
+        greet(zz, q_prev * 2 + 1, dp)
+        greet(zz, q_next * 2, dp)
+    greet(z, mate, dp)
+    ny = 2 * ndp
+    nx = plane // ny
+
+    def in_plane(dx, dy):
+        xx = lax.rem(q // 2 + dx, nx)
+        yy = lax.rem(dp * 2 + q % 2 + dy, ny)
+        return z, (xx * 2 + yy % 2) * 2 + core, yy // 2
+
+    steps = ((1, 0), (nx - 1, 0), (0, 1), (0, ny - 1))
+    for step in steps:
+        greet(*in_plane(*step))
+
     pl.semaphore_wait(barrier, len(greeted))
+    for load in loads[:2]:
+        load.wait()
 
     far = lax.rem(q + nq - 1 + 2 * core, nq)
     edge_cols = pl.ds(pl.multiple_of(core * (cols - side), 16), side)
     near_cols = pl.ds(pl.multiple_of((1 - core) * (cols - side), 16), side)
+    win_cols = pl.ds(pl.multiple_of(side + core * (cols - side), 16), side)
     started = []
 
     def send(src, dst, slots, zz, ll):
@@ -94,24 +106,25 @@
     lat_sides = ((up, rows - 1, 0, 0), (down, 0, rows + 1, 1))
     for zz, row, place, which in lat_sides:
         for cc in range(2):
-            send(field_hbm.at[0, row], win.at[core, place, inside[1]],
+            send(win.at[core, row + 1, inside[1]], win.at[core, place, inside[1]],
                  (which * 2 + cc, which * 2 + core), zz, q * 2 + cc)
     for zz, row, place, which in lat_sides:
         for cc in range(2):
-            send(field_hbm.at[0, row, edge_cols], edge.at[1 - core, place],
+            send(win.at[core, row + 1, win_cols], edge.at[1 - core, place],
                  (6 + which * 2 + cc, 6 + which * 2 + 1 - core), zz, far * 2 + cc)
     for cc in range(2):
-        send(field_hbm.at[0, :, edge_cols], edge.at[1 - core, inside[0]],
+        send(win.at[core, inside[0], win_cols], edge.at[1 - core, inside[0]],
              (4 + cc, 4 + 1 - core), z, far * 2 + cc)
-    send(field_hbm.at[0], win.at[core, inside[0], inside[1]], (10, 10), z, mate)
-    send(cot_hbm.at[0], cot.at[core], (11, 11), z, mate)
+    own = win.at[core, inside[0], inside[1]]
+    send(own, own, (10, 10), z, mate)
+    send(cot.at[core], cot.at[core], (11, 11), z, mate)
     for zz, row, place, which in lat_sides:
-        send(cot_hbm.at[0, row], cwin.at[place, inside[1]], (12 + which, 12 + which), zz, lon)
-        send(cot_hbm.at[0, row, near_cols], cedge.at[core, place], (14 + which, 14 + which),
+        send(cot.at[core, row], cwin.at[place, inside[1]], (12 + which, 12 + which), zz, lon)
+        send(cot.at[core, row, near_cols], cedge.at[core, place], (14 + which, 14 + which),
              zz, mate)
-        send(cot_hbm.at[0, row, edge_cols], cedge.at[1 - core, place], (16 + which, 16 + which),
+        send(cot.at[core, row, edge_cols], cedge.at[1 - core, place], (16 + which, 16 + which),
              zz, far * 2 + 1 - core)
-    send(cot_hbm.at[0, :, edge_cols], cedge.at[1 - core, inside[0]], (18, 18),
+    send(cot.at[core, :, edge_cols], cedge.at[1 - core, inside[0]], (18, 18),
          z, far * 2 + 1 - core)
 
     def arrived(slot, like):
@@ -131,6 +144,17 @@
         for way in range(2):
             pl.semaphore_wait(near_sem.at[n, way], 1)
 
+    def tell_plane(far_steps, base):
+        for n, step in enumerate(far_steps):
+            pl.semaphore_signal(plane_sem.at[base + n], inc=1, device_id=device(*in_plane(*step)),
+                                device_id_type=MESH)
+
+    def told_plane(far_steps, base):
+        for n in range(len(far_steps)):
+            pl.semaphore_wait(plane_sem.at[base + n], 1)
+
+    jumps = [step for step, size in (((2, 0), nx), ((0, 2), ny)) if size > 2]
+
     def relay(n):
         if 0 < n <= len(spans):
             told(n - 1)
@@ -138,6 +162,7 @@
             tell(n)
 
     relay(0)
+    tell_plane(steps, 0)
 
     lanes = 3 * block + side
     tap_lane = lax.broadcasted_iota(jnp.int32, (taps, lanes), 0)
@@ -169,8 +194,10 @@
     for load in small_loads:
         load.wait()
     make_band(fband, False)
-
-    for load in loads:
+    told_plane(steps, 0)
+    tell_plane(jumps, len(steps))
+
+    for load in loads[2:]:
         load.wait()
     arrived(11, cot.at[0])
     for s in range(2):
@@ -226,6 +253,7 @@
             conv[:, s * rows + i] = part.astype(BF16).reshape(basis, cols, chans)
 
     mine_t = cot_t[:, core].reshape(nq * blk, 2 * rows * cols)
+    told_plane(jumps, len(steps))
     groups = [range(n, min(n + GROUP, basis)) for n in range(0, basis, GROUP)]
     a_copies = []
     for n, group in enumerate(groups):
@@ -316,44 +344,6 @@
                     recv_sem=b_rsem.at[z], device_id=device(keeper(k), lon, dp),
                     device_id_type=MESH).start()
 
-    my_k = jnp.int32(basis)
-    for k in range(basis):
-        my_k = jnp.where(z == keeper(k), k, my_k)
-    keeps = my_k < basis
-    my_k = jnp.minimum(my_k, basis - 1)
-    my_lanes = pl.ds(pl.multiple_of(dp * half, half), half)
-    pl.semaphore_wait(dp_sem, 1)
-
-    @pl.when(keeps)
-    def _():
-        for r in range(1, nz):
-            place = lax.rem(z + r, nz)
-            pltpu.make_async_copy(b_recv.at[place], b_recv.at[place], b_rsem.at[place]).wait()
-        b_recv[z] = b_send[my_k]
-        summed = jnp.zeros((blk, half), F32)
-        for r in range(nz):
-            summed = summed + b_recv[r].astype(F32)
-        c_send[...] = (summed * scale).astype(BF16)
-        for zz in sorted(range(nz), key=lambda zz: (zz + nz // 2 + 1) % nz, reverse=True):
-            for dd in range(ndp):
-                @pl.when(jnp.logical_or(z != zz, dp != dd))
-                def _(zz=zz, dd=dd):
-                    pltpu.make_async_remote_copy(
-                        src_ref=c_send, dst_ref=final.at[my_k, :, my_lanes],
-                        send_sem=c_ssem.at[dd * nz + zz], recv_sem=c_rsem.at[my_k * ndp + dp],
-                        device_id=device(zz, lon, dd), device_id_type=MESH).start()
-        final[my_k, :, my_lanes] = c_send[...]
-
-    for k in range(basis):
-        for h in range(ndp):
-            @pl.when(jnp.logical_or(z != keeper(k), dp != h))
-            def _(k=k, h=h):
-                spot = final.at[k, :, pl.ds(h * half, half)]
-                pltpu.make_async_copy(spot, spot, c_rsem.at[k * ndp + h]).wait()
-
-    gw_copy = pltpu.make_async_copy(final, gw_hbm, local_sem.at[2])
-    gw_copy.start()
-
     for copy in started:
         copy.wait_send()
     for copies in a_copies:
@@ -363,6 +353,44 @@
         @pl.when(z != keeper(k))
         def _(k=k):
             pltpu.make_async_copy(b_send.at[k], b_send.at[k], b_ssem.at[k]).wait()
+
+    my_k = jnp.int32(basis)
+    for k in range(basis):
+        my_k = jnp.where(z == keeper(k), k, my_k)
+    keeps = my_k < basis
+    my_k = jnp.minimum(my_k, basis - 1)
+    my_lanes = pl.ds(pl.multiple_of(dp * half, half), half)
+    pl.semaphore_wait(dp_sem, 1)
+
+    @pl.when(keeps)
+    def _():
+        for r in range(1, nz):
+            place = lax.rem(z + r, nz)
+            pltpu.make_async_copy(b_recv.at[place], b_recv.at[place], b_rsem.at[place]).wait()
+        b_recv[z] = b_send[my_k]
+        summed = jnp.zeros((blk, half), F32)
+        for r in range(nz):
+            summed = summed + b_recv[r].astype(F32)
+        c_send[...] = (summed * scale).astype(BF16)
+        for zz in range(nz):
+            for dd in range(ndp):
+                @pl.when(jnp.logical_or(z != zz, dp != dd))
+                def _(zz=zz, dd=dd):
+                    pltpu.make_async_remote_copy(
+                        src_ref=c_send, dst_ref=final.at[my_k, :, my_lanes],
+                        send_sem=c_ssem.at[dd * nz + zz], recv_sem=c_rsem.at[my_k * ndp + dp],
+                        device_id=device(zz, lon, dd), device_id_type=MESH).start()
+        final[my_k, :, my_lanes] = c_send[...]
+
+    for k in range(basis):
+        for h in range(ndp):
+            @pl.when(jnp.logical_or(z != keeper(k), dp != h))
+            def _(k=k, h=h):
+                spot = final.at[k, :, pl.ds(h * half, half)]
+                pltpu.make_async_copy(spot, spot, c_rsem.at[k * ndp + h]).wait()
+
+    gw_copy = pltpu.make_async_copy(final, gw_hbm, local_sem.at[2])
+    gw_copy.start()
 
     @pl.when(keeps)
     def _():
@@ -438,7 +466,8 @@
             pltpu.VMEM((blk, half), BF16),
             dma((6,)), dma((19,)), dma((19,)), dma((groups, plane - 1)), dma((groups, plane - 1)),
             dma((basis,)), dma((nz,)), dma((nz * ndp,)), dma((basis * ndp,)),
-            pltpu.SemaphoreType.REGULAR((4, 2)), pltpu.SemaphoreType.REGULAR,
+            pltpu.SemaphoreType.REGULAR((4, 2)), pltpu.SemaphoreType.REGULAR((6,)),
+            pltpu.SemaphoreType.REGULAR,
         ],
         compiler_params=pltpu.CompilerParams(
             collective_id=0, has_side_effects=True),

time: 51.5 us -> 49.1 us (0.953)
  the two profiles are of different devices: /device:TPU:1 before, /device:TPU:64 now
where the time goes in v4:
time: 49.1 us; the launch traced here: 48.9 us
  Pallas kernels  46.1 us (94%)
  local copies, waits for them, and re-layouts  2.14 us (4%)
  between operations  0.66 us (1%)
    pallas_call x1, Pallas kernels, on_device(): pl.pallas_call(functools.partial(kernel_body, sizes), out_shape=shapes, i...  44.4 us
    unnamed x3, local copies, waits for them, and re-layouts  1.99 us
    pallas_call x1, Pallas kernels, on_device(): pl.pallas_call(hand_over, out_shape=shapes, in_specs=[vmem] * 3, out_spec...  1.76 us

profile of v4, /device:TPU:64, one launch (start us, length us, event | category | flops | bytes accessed | tf_op | source)
XLA Modules:
  0.0 48.9 jit_solution(9715896391455584021)
XLA Ops:
  0.6 0.0 copy-start
  0.7 0.9 %copy-done = bf16[9,64,3,17]{1,2,3,0:T(4,128)(2,1)S(1)} copy-done((bf16[9,64,3,17]{1,2,3,0:T(4,128)(2,1)S(1)}, bf16[9,64,3,17]{1,2,3,0:T(4,128)(2,1)}, u32[]{:S(2)}) %copy-start) | copy-done | bytes 58776
  1.5 0.2 constant_dynamic-slice_fusion
  1.7 1.1 %copy.9 = bf16[9,6,3,17]{3,0,1,2:T(8,128)(2,1)} copy(bf16[9,6,3,17]{1,2,3,0:T(4,128)(2,1)S(1)} %constant_dynamic-slice_fusion) | data formatting | bytes 11016
  2.8 44.4 %disco_block.1 = (bf16[1,4,64,256]{3,2,1,0:T(8,128)(2,1)}, bf16[1,4,64,256]{3,2,1,0:T(8,128)(2,1)}, bf16[9,16,256]{2,1,0:T(8,128)(2,1)}) custom-call(bf16[3,6,9,17]{3,2,1,0:T(8,128)(2,1)} %bitcast.2, s32[64]{0:T(128)} %reach_hbm.1, bf16[1,4,64,256]{3,2,1,0:T(8,128)(2,1)} %field_hbm.1, bf16[1,4,64,256]{3,2,1,0:T(8,128)(2,1)} %cot_hbm.1, ...), custom_call_target="tpu_custom_call" | custom-call | tf_op jit(solution)/shard_map/disco_block/pallas_call | solution.py:441
  47.2 1.8 %hand_over.1 = (bf16[1,4,64,256]{3,2,1,0:T(8,128)(2,1)}, bf16[1,4,64,256]{3,2,1,0:T(8,128)(2,1)}, bf16[9,16,256]{2,1,0:T(8,128)(2,1)}) custom-call(bf16[1,4,64,256]{3,2,1,0:T(8,128)(2,1)} %get-tuple-element.9.refs_0_, bf16[1,4,64,256]{3,2,1,0:T(8,128)(2,1)} %get-tuple-element.10.refs_1_, bf16[9,16,256]{2,1,0:T(8,128)(2,1)} %get-tuple-element.11.refs_2_), custom_call_target="tpu_custom_call" | custom-call | tf_op jit(solution)/shard_map/hand_over/pallas_call | solution.py:477
Async XLA Ops:
  0.6 0.9 %copy-start = (bf16[9,64,3,17]{1,2,3,0:T(4,128)(2,1)S(1)}, bf16[9,64,3,17]{1,2,3,0:T(4,128)(2,1)}, u32[]{:S(2)}) copy-start(bf16[9,64,3,17]{1,2,3,0:T(4,128)(2,1)} %param.8) | copy-start | bytes 176260

commit v5 on v4

--- a/solution.py
+++ b/solution.py
@@ -106,15 +106,15 @@
     lat_sides = ((up, rows - 1, 0, 0), (down, 0, rows + 1, 1))
     for zz, row, place, which in lat_sides:
         for cc in range(2):
-            send(win.at[core, row + 1, inside[1]], win.at[core, place, inside[1]],
-                 (which * 2 + cc, which * 2 + core), zz, q * 2 + cc)
-    for zz, row, place, which in lat_sides:
-        for cc in range(2):
             send(win.at[core, row + 1, win_cols], edge.at[1 - core, place],
                  (6 + which * 2 + cc, 6 + which * 2 + 1 - core), zz, far * 2 + cc)
     for cc in range(2):
         send(win.at[core, inside[0], win_cols], edge.at[1 - core, inside[0]],
              (4 + cc, 4 + 1 - core), z, far * 2 + cc)
+    for zz, row, place, which in lat_sides:
+        for cc in range(2):
+            send(win.at[core, row + 1, inside[1]], win.at[core, place, inside[1]],
+                 (which * 2 + cc, which * 2 + core), zz, q * 2 + cc)
     own = win.at[core, inside[0], inside[1]]
     send(own, own, (10, 10), z, mate)
     send(cot.at[core], cot.at[core], (11, 11), z, mate)
@@ -373,7 +373,7 @@
             summed = summed + b_recv[r].astype(F32)
         c_send[...] = (summed * scale).astype(BF16)
         for zz in range(nz):
-            for dd in range(ndp):
+            for dd in [(dp + 1 + n) % ndp for n in range(ndp)]:
                 @pl.when(jnp.logical_or(z != zz, dp != dd))
                 def _(zz=zz, dd=dd):
                     pltpu.make_async_remote_copy(

time: 49.1 us -> 48.5 us (0.988)
  the two profiles are of different devices: /device:TPU:64 before, /device:TPU:1 now
where the time goes in v5:
time: 48.5 us; the launch traced here: 47.6 us
  Pallas kernels  44.8 us (92%)
  local copies, waits for them, and re-layouts  2.14 us (4%)
  between operations  0.66 us (1%)
    pallas_call x1, Pallas kernels, on_device(): pl.pallas_call(functools.partial(kernel_body, sizes), out_shape=shapes, i...  43 us
    unnamed x3, local copies, waits for them, and re-layouts  1.99 us
    pallas_call x1, Pallas kernels, on_device(): pl.pallas_call(hand_over, out_shape=shapes, in_specs=[vmem] * 3, out_spec...  1.76 us

profile of v5, /device:TPU:1, one launch (start us, length us, event | category | flops | bytes accessed | tf_op | source)
XLA Modules:
  0.0 47.6 jit_solution(3722288066729076955)
XLA Ops:
  0.6 0.0 copy-start
  0.7 0.9 %copy-done = bf16[9,64,3,17]{1,2,3,0:T(4,128)(2,1)S(1)} copy-done((bf16[9,64,3,17]{1,2,3,0:T(4,128)(2,1)S(1)}, bf16[9,64,3,17]{1,2,3,0:T(4,128)(2,1)}, u32[]{:S(2)}) %copy-start) | copy-done | bytes 58776
  1.5 0.2 constant_dynamic-slice_fusion
  1.7 1.1 %copy.9 = bf16[9,6,3,17]{3,0,1,2:T(8,128)(2,1)} copy(bf16[9,6,3,17]{1,2,3,0:T(4,128)(2,1)S(1)} %constant_dynamic-slice_fusion) | data formatting | bytes 11016
  2.8 43.0 %disco_block.1 = (bf16[1,4,64,256]{3,2,1,0:T(8,128)(2,1)}, bf16[1,4,64,256]{3,2,1,0:T(8,128)(2,1)}, bf16[9,16,256]{2,1,0:T(8,128)(2,1)}) custom-call(bf16[3,6,9,17]{3,2,1,0:T(8,128)(2,1)} %bitcast.2, s32[64]{0:T(128)} %reach_hbm.1, bf16[1,4,64,256]{3,2,1,0:T(8,128)(2,1)} %field_hbm.1, bf16[1,4,64,256]{3,2,1,0:T(8,128)(2,1)} %cot_hbm.1, ...), custom_call_target="tpu_custom_call" | custom-call | tf_op jit(solution)/shard_map/disco_block/pallas_call | solution.py:441
  45.8 1.8 %hand_over.1 = (bf16[1,4,64,256]{3,2,1,0:T(8,128)(2,1)}, bf16[1,4,64,256]{3,2,1,0:T(8,128)(2,1)}, bf16[9,16,256]{2,1,0:T(8,128)(2,1)}) custom-call(bf16[1,4,64,256]{3,2,1,0:T(8,128)(2,1)} %get-tuple-element.9.refs_0_, bf16[1,4,64,256]{3,2,1,0:T(8,128)(2,1)} %get-tuple-element.10.refs_1_, bf16[9,16,256]{2,1,0:T(8,128)(2,1)} %get-tuple-element.11.refs_2_), custom_call_target="tpu_custom_call" | custom-call | tf_op jit(solution)/shard_map/hand_over/pallas_call | solution.py:477
Async XLA Ops:
  0.6 0.9 %copy-start = (bf16[9,64,3,17]{1,2,3,0:T(4,128)(2,1)S(1)}, bf16[9,64,3,17]{1,2,3,0:T(4,128)(2,1)}, u32[]{:S(2)}) copy-start(bf16[9,64,3,17]{1,2,3,0:T(4,128)(2,1)} %param.8) | copy-start | bytes 176260

commit v6 on v5

--- a/solution.py
+++ b/solution.py
@@ -41,20 +41,6 @@
     def device(zz, ll, dd):
         return {"lat": zz, "lon": ll, "dp": dd}
 
-    inside = (pl.ds(1, rows), pl.ds(side, cols))
-    loads = [
-        pltpu.make_async_copy(field_hbm.at[0], win.at[core, inside[0], inside[1]], local_sem.at[0]),
-        pltpu.make_async_copy(cot_hbm.at[0], cot.at[core], local_sem.at[1]),
-        pltpu.make_async_copy(cot_hbm.at[0], cwin.at[inside[0], inside[1]], local_sem.at[2]),
-        pltpu.make_async_copy(weight_hbm, weight, local_sem.at[3]),
-    ]
-    small_loads = [
-        pltpu.make_async_copy(coeff_hbm, coeff, local_sem.at[4]),
-        pltpu.make_async_copy(reach_hbm, reach_cols, local_sem.at[5]),
-    ]
-    for load in small_loads + loads:
-        load.start()
-
     barrier = pltpu.get_barrier_semaphore()
     greeted = []
 
@@ -85,6 +71,20 @@
     steps = ((1, 0), (nx - 1, 0), (0, 1), (0, ny - 1))
     for step in steps:
         greet(*in_plane(*step))
+
+    inside = (pl.ds(1, rows), pl.ds(side, cols))
+    loads = [
+        pltpu.make_async_copy(field_hbm.at[0], win.at[core, inside[0], inside[1]], local_sem.at[0]),
+        pltpu.make_async_copy(cot_hbm.at[0], cot.at[core], local_sem.at[1]),
+        pltpu.make_async_copy(cot_hbm.at[0], cwin.at[inside[0], inside[1]], local_sem.at[2]),
+        pltpu.make_async_copy(weight_hbm, weight, local_sem.at[3]),
+    ]
+    small_loads = [
+        pltpu.make_async_copy(coeff_hbm, coeff, local_sem.at[4]),
+        pltpu.make_async_copy(reach_hbm, reach_cols, local_sem.at[5]),
+    ]
+    for load in loads[:2] + small_loads + loads[2:3]:
+        load.start()
 
     pl.semaphore_wait(barrier, len(greeted))
     for load in loads[:2]:
@@ -161,6 +161,7 @@
         if n < len(spans):
             tell(n)
 
+    loads[3].start()
     relay(0)
     tell_plane(steps, 0)
 

time: 48.5 us -> 48.5 us (level)
  no operation moved by 1% of the time
where the time goes in v6:
time: 48.5 us; the launch traced here: 47.6 us
  Pallas kernels  44.8 us (92%)
  local copies, waits for them, and re-layouts  2.14 us (4%)
  between operations  0.66 us (1%)
    pallas_call x1, Pallas kernels, on_device(): pl.pallas_call(functools.partial(kernel_body, sizes), out_shape=shapes, i...  43 us
    unnamed x3, local copies, waits for them, and re-layouts  1.99 us
    pallas_call x1, Pallas kernels, on_device(): pl.pallas_call(hand_over, out_shape=shapes, in_specs=[vmem] * 3, out_spec...  1.76 us

profile of v6, /device:TPU:1, one launch (start us, length us, event | category | flops | bytes accessed | tf_op | source)
XLA Modules:
  0.0 47.6 jit_solution(5130795561092030401)
XLA Ops:
  0.6 0.0 copy-start
  0.7 0.9 %copy-done = bf16[9,64,3,17]{1,2,3,0:T(4,128)(2,1)S(1)} copy-done((bf16[9,64,3,17]{1,2,3,0:T(4,128)(2,1)S(1)}, bf16[9,64,3,17]{1,2,3,0:T(4,128)(2,1)}, u32[]{:S(2)}) %copy-start) | copy-done | bytes 58776
  1.5 0.2 constant_dynamic-slice_fusion
  1.7 1.1 %copy.9 = bf16[9,6,3,17]{3,0,1,2:T(8,128)(2,1)} copy(bf16[9,6,3,17]{1,2,3,0:T(4,128)(2,1)S(1)} %constant_dynamic-slice_fusion) | data formatting | bytes 11016
  2.8 43.0 %disco_block.1 = (bf16[1,4,64,256]{3,2,1,0:T(8,128)(2,1)}, bf16[1,4,64,256]{3,2,1,0:T(8,128)(2,1)}, bf16[9,16,256]{2,1,0:T(8,128)(2,1)}) custom-call(bf16[3,6,9,17]{3,2,1,0:T(8,128)(2,1)} %bitcast.2, s32[64]{0:T(128)} %reach_hbm.1, bf16[1,4,64,256]{3,2,1,0:T(8,128)(2,1)} %field_hbm.1, bf16[1,4,64,256]{3,2,1,0:T(8,128)(2,1)} %cot_hbm.1, ...), custom_call_target="tpu_custom_call" | custom-call | tf_op jit(solution)/shard_map/disco_block/pallas_call | solution.py:442
  45.8 1.8 %hand_over.1 = (bf16[1,4,64,256]{3,2,1,0:T(8,128)(2,1)}, bf16[1,4,64,256]{3,2,1,0:T(8,128)(2,1)}, bf16[9,16,256]{2,1,0:T(8,128)(2,1)}) custom-call(bf16[1,4,64,256]{3,2,1,0:T(8,128)(2,1)} %get-tuple-element.9.refs_0_, bf16[1,4,64,256]{3,2,1,0:T(8,128)(2,1)} %get-tuple-element.10.refs_1_, bf16[9,16,256]{2,1,0:T(8,128)(2,1)} %get-tuple-element.11.refs_2_), custom_call_target="tpu_custom_call" | custom-call | tf_op jit(solution)/shard_map/hand_over/pallas_call | solution.py:478
Async XLA Ops:
  0.6 0.9 %copy-start = (bf16[9,64,3,17]{1,2,3,0:T(4,128)(2,1)S(1)}, bf16[9,64,3,17]{1,2,3,0:T(4,128)(2,1)}, u32[]{:S(2)}) copy-start(bf16[9,64,3,17]{1,2,3,0:T(4,128)(2,1)} %param.8) | copy-start | bytes 176260
